TPU v7x, 32 devices: a whole 2x2x4 slice. The times are simulated.
32 devices in a mesh: seq: 8 (over z, x), tp: 4 (over y, core).
Axes of the slice: x: 2, y: 2, z: 4, core: 2. Of those that a mesh axis runs over, the one named last changes fastest.
Arguments:
- tokens: bfloat16 [4096, 768], P(('seq', 'tp')), may hold values from -6 to 6
- cotangent: bfloat16 [4096, 768], P(('seq', 'tp')), may hold values from -6 to 6
- prefix_length: int32 [1], replicated, may hold values from 0 to 2047
- mask_flags: int32 [4096], P(('seq', 'tp')), may hold values 0 or 1
- timestep: int32 [1], replicated, may hold values from 0 to 999
- mask_embed: bfloat16 [768], replicated, may hold values from -6 to 6
- ln1_gain: bfloat16 [768], replicated, may hold values from 0.099609375 to 1.8984375
- ln2_gain: bfloat16 [768], replicated, may hold values from 0.099609375 to 1.8984375
- ada_weight: bfloat16 [128, 4608], replicated, may hold values from -0.5 to 0.5
- ada_bias: bfloat16 [4608], replicated, may hold values from -3 to 3
- qkv_weight: bfloat16 [768, 2304], replicated, may hold values from -0.21875 to 0.21875
- out_weight: bfloat16 [768, 768], replicated, may hold values from -2 to 2
- up_weight: bfloat16 [768, 3072], P(None, 'tp'), may hold values from -0.21875 to 0.21875
- up_bias: bfloat16 [3072], P('tp'), may hold values from -3 to 3
- down_weight: bfloat16 [3072, 768], P('tp'), may hold values from -0.109375 to 0.109375
- down_bias: bfloat16 [768], replicated, may hold values from -3 to 3
Outputs:
- output: bfloat16 [4096, 768], P(('seq', 'tp'))
- input_grad: float32 [4096, 768], P(('seq', 'tp'))
- mask_embed_grad: float32 [768], replicated
- ln1_gain_grad: float32 [768], replicated
- ln2_gain_grad: float32 [768], replicated
- ada_weight_grad: float32 [128, 4608], replicated
- ada_bias_grad: float32 [4608], replicated
- qkv_weight_grad: float32 [768, 2304], replicated
- out_weight_grad: float32 [768, 768], replicated
- up_weight_grad: float32 [768, 3072], P(None, 'tp')
- up_bias_grad: float32 [3072], P('tp')
- down_weight_grad: float32 [3072, 768], P('tp')
- down_bias_grad: float32 [768], replicated
All inputs are finite; a program needn't handle non-finite values. No bound on the sum of `mask_flags` on one device may be relied on, other than what follows from the above.
Results may differ from a plain program's by a relative error of at most 0.019.
Values may be sent and summed in bfloat16 or wider, within the bound.
A program may use at most 384 MiB of HBM per device.

v0:
```python
import math

import jax
import jax.numpy as jnp
from jax import lax
from jax.sharding import PartitionSpec as P

HEADS = 12


epsilon = 1e-05
highest = lax.Precision.HIGHEST
floor_value = -1e30


def layer_norm(inputs, norm_gain):
    centred = inputs - jnp.mean(inputs, axis=-1, keepdims=True)
    variance = jnp.mean(centred * centred, axis=-1, keepdims=True)
    return centred * lax.rsqrt(variance + epsilon) * norm_gain


def modulate(inputs, norm_gain, shift_vector, scale_vector):
    return layer_norm(inputs, norm_gain) * (1.0 + scale_vector) + shift_vector


def rotary_tables(positions, head_width):
    halfway = head_width // 2
    inverse = jnp.exp(-math.log(10000.0) * jnp.arange(halfway, dtype=jnp.float32) / halfway)
    angles = positions.astype(jnp.float32)[:, None] * inverse[None, :]
    angles = jnp.concatenate([angles, angles], axis=1)
    return (jnp.cos(angles), jnp.sin(angles))


def rotate(head_rows, cosine, sine):
    halfway = head_rows.shape[-1] // 2
    turned = jnp.concatenate([-head_rows[..., halfway:], head_rows[..., :halfway]], axis=-1)
    return head_rows * cosine[:, None, :] + turned * sine[:, None, :]


def time_embedding(timestep, embed_width):
    halfway = embed_width // 2
    rates = jnp.exp(-math.log(10000.0) * jnp.arange(halfway, dtype=jnp.float32) / halfway)
    angles = timestep[0].astype(jnp.float32) * rates
    return jnp.concatenate([jnp.cos(angles), jnp.sin(angles)])


def block_length(total_rows, other_count):
    pieces = total_rows // other_count
    widest = 1 << max(0, (2048 // other_count).bit_length() - 1)
    size = other_count * math.gcd(pieces, widest)
    return size


def over_blocks(running, row_arrays, other_count, advance):
    total_rows = row_arrays[0].shape[0]
    block_size = block_length(total_rows, other_count)

    def one_turn(block_index, current):
        block_start = block_index * block_size
        blocks = tuple(
            (lax.dynamic_slice_in_dim(array, block_start, block_size, 0) for array in row_arrays)
        )
        return advance(current, blocks)

    return lax.fori_loop(0, total_rows // block_size, one_turn, running)


def forward_update(running, queries, key_block, value_block, score_scale):
    highest_seen, totals, weighted = running
    scores = (
        jnp.einsum("qhd,khd->hqk", queries, key_block, preferred_element_type=jnp.float32)
        * score_scale
    )
    new_highest = jnp.maximum(highest_seen, jnp.max(scores, axis=-1))
    factor = jnp.exp(highest_seen - new_highest)
    weights = jnp.exp(scores - new_highest[:, :, None])
    totals = totals * factor + jnp.sum(weights, axis=-1)
    weighted = weighted * factor.T[:, :, None] + jnp.einsum(
        "hqk,khd->qhd",
        weights.astype(jnp.bfloat16),
        value_block,
        preferred_element_type=jnp.float32,
    )
    return (new_highest, totals, weighted)


def query_update(
    query_grad, queries, mixed_grad, logsum, delta, key_block, value_block, score_scale
):
    scores = (
        jnp.einsum("qhd,khd->hqk", queries, key_block, preferred_element_type=jnp.float32)
        * score_scale
    )
    probs = jnp.exp(scores - logsum[:, :, None])
    prob_grad = jnp.einsum(
        "qhd,khd->hqk", mixed_grad, value_block, preferred_element_type=jnp.float32
    )
    score_grad = (probs * (prob_grad - delta[:, :, None])).astype(jnp.bfloat16)
    return query_grad + score_scale * jnp.einsum(
        "hqk,khd->qhd", score_grad, key_block, preferred_element_type=jnp.float32
    )


def key_update(
    running, query_block, grad_block, logsum_block, delta_block, own_keys, own_values, score_scale
):
    key_grad, value_grad = running
    scores = (
        jnp.einsum("qhd,khd->hqk", query_block, own_keys, preferred_element_type=jnp.float32)
        * score_scale
    )
    probs = jnp.exp(scores - logsum_block.T[:, :, None])
    value_grad = value_grad + jnp.einsum(
        "hqk,qhd->khd", probs.astype(jnp.bfloat16), grad_block, preferred_element_type=jnp.float32
    )
    prob_grad = jnp.einsum(
        "qhd,khd->hqk", grad_block, own_values, preferred_element_type=jnp.float32
    )
    score_grad = (probs * (prob_grad - delta_block.T[:, :, None])).astype(jnp.bfloat16)
    key_grad = key_grad + score_scale * jnp.einsum(
        "hqk,qhd->khd", score_grad, query_block, preferred_element_type=jnp.float32
    )
    return (key_grad, value_grad)


def per_device(
    tokens,
    cotangent,
    prefix_length,
    mask_flags,
    timestep,
    mask_embed,
    ln1_gain,
    ln2_gain,
    ada_weight,
    ada_bias,
    qkv_weight,
    out_weight,
    up_weight,
    up_bias,
    down_weight,
    down_bias,
):
    row_count = tokens.shape[0]
    model_width = tokens.shape[1]
    head_count = HEADS
    head_width = model_width // head_count
    score_scale = head_width ** (-0.5)
    positions = lax.axis_index(("seq", "tp")) * row_count + jnp.arange(row_count, dtype=jnp.int32)
    masked = ((positions >= prefix_length[0]) & (mask_flags == 1)).astype(jnp.float32)
    activation = jax.nn.silu(time_embedding(timestep, ada_weight.shape[0]))
    modulation = jnp.dot(
        activation, ada_weight.astype(jnp.float32), precision=highest
    ) + ada_bias.astype(jnp.float32)
    shift_one, scale_one, gate_one, shift_two, scale_two, gate_two = jnp.split(modulation, 6)
    cosine, sine = rotary_tables(positions, head_width)
    gain_one = ln1_gain.astype(jnp.float32)
    gain_two = ln2_gain.astype(jnp.float32)
    start = tokens.astype(jnp.float32) + masked[:, None] * mask_embed.astype(jnp.float32)[None, :]
    normed = modulate(start, gain_one, shift_one, scale_one).astype(jnp.bfloat16)
    projected = jnp.dot(normed, qkv_weight, preferred_element_type=jnp.float32)
    split_rows = projected.reshape(row_count, 3, head_count, head_width)
    queries = rotate(split_rows[:, 0], cosine, sine).astype(jnp.bfloat16)
    key_rows = (
        rotate(split_rows[:, 1], cosine, sine).reshape(row_count, model_width).astype(jnp.bfloat16)
    )
    value_rows = projected[:, 2 * model_width :].astype(jnp.bfloat16)
    initial = (
        jnp.full((head_count, row_count), floor_value, jnp.float32),
        jnp.zeros((head_count, row_count), jnp.float32),
        jnp.zeros((row_count, head_count, head_width), jnp.float32),
    )

    def advance(current, blocks):
        return forward_update(
            current,
            queries,
            blocks[0].reshape(-1, head_count, head_width),
            blocks[1].reshape(-1, head_count, head_width),
            score_scale,
        )

    running = over_blocks(
        initial,
        (
            lax.all_gather(key_rows, ("seq", "tp"), axis=0, tiled=True),
            lax.all_gather(value_rows, ("seq", "tp"), axis=0, tiled=True),
        ),
        row_count,
        advance,
    )
    highest_seen, totals, weighted = running
    logsum = highest_seen + jnp.log(totals)
    attended = weighted / totals.T[:, :, None]
    mixed = attended.reshape(row_count, model_width).astype(jnp.bfloat16)
    branch = jnp.dot(mixed, out_weight, preferred_element_type=jnp.float32)
    middle = start + gate_one * branch
    normed_two = modulate(middle, gain_two, shift_two, scale_two).astype(jnp.bfloat16)
    group_rows = lax.all_gather(normed_two, "tp", axis=0, tiled=True)
    hidden = jnp.dot(group_rows, up_weight, preferred_element_type=jnp.float32) + up_bias.astype(
        jnp.float32
    )
    active = jax.nn.gelu(hidden).astype(jnp.bfloat16)
    result = lax.psum_scatter(
        jnp.dot(active, down_weight, preferred_element_type=jnp.float32).astype(jnp.bfloat16),
        "tp",
        scatter_dimension=0,
        tiled=True,
    ).astype(jnp.float32) + down_bias.astype(jnp.float32)
    output = (middle + gate_two * result).astype(jnp.bfloat16)
    upstream = cotangent.astype(jnp.float32)
    result_grad = (upstream * gate_two).astype(jnp.bfloat16)
    gate_two_grad = jnp.sum(upstream * result, axis=0)
    down_bias_grad = jnp.sum(result_grad.astype(jnp.float32), axis=0)
    group_grads = lax.all_gather(result_grad, "tp", axis=0, tiled=True)
    down_weight_grad = jnp.dot(active.T, group_grads, preferred_element_type=jnp.float32)
    active_grad = jnp.dot(group_grads, down_weight.T, preferred_element_type=jnp.float32)
    unused, gelu_back = jax.vjp(jax.nn.gelu, hidden)
    hidden_grad = gelu_back(active_grad)[0].astype(jnp.bfloat16)
    up_bias_grad = jnp.sum(hidden_grad.astype(jnp.float32), axis=0)
    up_weight_grad = jnp.dot(group_rows.T, hidden_grad, preferred_element_type=jnp.float32)
    normed_two_grad = lax.psum_scatter(
        jnp.dot(hidden_grad, up_weight.T, preferred_element_type=jnp.float32).astype(jnp.bfloat16),
        "tp",
        scatter_dimension=0,
        tiled=True,
    ).astype(jnp.float32)
    unused, second_back = jax.vjp(modulate, middle, gain_two, shift_two, scale_two)
    middle_part, gain_two_grad, shift_two_grad, scale_two_grad = second_back(normed_two_grad)
    middle_grad = middle_part + upstream
    gate_one_grad = jnp.sum(middle_grad * branch, axis=0)
    branch_grad = (middle_grad * gate_one).astype(jnp.bfloat16)
    out_weight_grad = jnp.dot(mixed.T, branch_grad, preferred_element_type=jnp.float32)
    mixed_grad = (
        jnp.dot(branch_grad, out_weight.T, preferred_element_type=jnp.float32)
        .astype(jnp.bfloat16)
        .reshape(row_count, head_count, head_width)
    )
    delta_rows = jnp.sum(mixed_grad.astype(jnp.float32) * attended, axis=-1)
    delta = delta_rows.T
    initial_query = jnp.zeros((row_count, head_count, head_width), jnp.float32)

    def advance(grads_now, blocks):
        return query_update(
            grads_now,
            queries,
            mixed_grad,
            logsum,
            delta,
            blocks[0].reshape(-1, head_count, head_width),
            blocks[1].reshape(-1, head_count, head_width),
            score_scale,
        )

    query_grad = over_blocks(
        initial_query,
        (
            lax.all_gather(key_rows, ("seq", "tp"), axis=0, tiled=True),
            lax.all_gather(value_rows, ("seq", "tp"), axis=0, tiled=True),
        ),
        row_count,
        advance,
    )
    every_logsum, every_delta = (
        lax.all_gather(logsum.T, ("seq", "tp"), axis=0, tiled=True),
        lax.all_gather(delta_rows, ("seq", "tp"), axis=0, tiled=True),
    )
    own_keys = key_rows.reshape(row_count, head_count, head_width)
    own_values = value_rows.reshape(row_count, head_count, head_width)
    initial_keys = (
        jnp.zeros((row_count, head_count, head_width), jnp.float32),
        jnp.zeros((row_count, head_count, head_width), jnp.float32),
    )

    def advance(grads_now, blocks):
        return key_update(
            grads_now, blocks[0], blocks[1], blocks[2], blocks[3], own_keys, own_values, score_scale
        )

    key_grad, value_grad = over_blocks(
        initial_keys,
        (
            lax.all_gather(queries, ("seq", "tp"), axis=0, tiled=True),
            lax.all_gather(mixed_grad, ("seq", "tp"), axis=0, tiled=True),
            every_logsum,
            every_delta,
        ),
        row_count,
        advance,
    )
    unused, rotate_back = jax.vjp(lambda head_rows: rotate(head_rows, cosine, sine), query_grad)
    query_part = rotate_back(query_grad)[0].reshape(row_count, model_width)
    key_part = rotate_back(key_grad)[0].reshape(row_count, model_width)
    projected_grad = jnp.concatenate(
        [query_part, key_part, value_grad.reshape(row_count, model_width)], axis=1
    ).astype(jnp.bfloat16)
    qkv_weight_grad = jnp.dot(normed.T, projected_grad, preferred_element_type=jnp.float32)
    normed_grad = jnp.dot(projected_grad, qkv_weight.T, preferred_element_type=jnp.float32)
    unused, first_back = jax.vjp(modulate, start, gain_one, shift_one, scale_one)
    start_part, gain_one_grad, shift_one_grad, scale_one_grad = first_back(normed_grad)
    start_grad = start_part + middle_grad
    embed_grad = jnp.sum(masked[:, None] * start_grad, axis=0)
    modulation_grad = jnp.concatenate(
        [
            shift_one_grad,
            scale_one_grad,
            gate_one_grad,
            shift_two_grad,
            scale_two_grad,
            gate_two_grad,
        ]
    )
    ada_weight_grad = activation[:, None] * modulation_grad[None, :]
    summed = lax.psum(
        (
            qkv_weight_grad,
            out_weight_grad,
            ada_weight_grad,
            modulation_grad,
            gain_one_grad,
            gain_two_grad,
            down_bias_grad,
            embed_grad,
        ),
        ("seq", "tp"),
    )
    split_sums = lax.psum((up_weight_grad, up_bias_grad, down_weight_grad), "seq")
    return (
        output,
        start_grad,
        summed[7],
        summed[4],
        summed[5],
        summed[2],
        summed[3],
        summed[0],
        summed[1],
        split_sums[0],
        split_sums[1],
        split_sums[2],
        summed[6],
    )


def solution(mesh):
    in_specs = (
        P(("seq", "tp"), None),
        P(("seq", "tp"), None),
        P(),
        P(("seq", "tp")),
        P(),
        P(),
        P(),
        P(),
        P(),
        P(),
        P(),
        P(),
        P(None, "tp"),
        P("tp"),
        P("tp", None),
        P(),
    )
    out_specs = (
        P(("seq", "tp"), None),
        P(("seq", "tp"), None),
        P(),
        P(),
        P(),
        P(),
        P(),
        P(),
        P(),
        P(None, "tp"),
        P("tp"),
        P("tp", None),
        P(),
    )
    return jax.shard_map(
        per_device, mesh=mesh, in_specs=in_specs, out_specs=out_specs, check_vma=False
    )
```

profile of v0, /device:TPU:0, one launch (start us, length us, event | category | flops | bytes accessed | tf_op | source)
XLA Modules:
  0.0 879.5 jit_solution(9662425984832255659)
XLA Ops:
  12.7 1.9 convolution_reduce_fusion
  16.6 1.7 fusion.112
  20.1 2.7 copy.38
  28.1 1.6 convert_reduce_fusion.2
  29.7 11.2 %all_gather.29 = bf16[512,768]{1,0:T(8,128)(2,1)S(1)} all-gather(bf16[128,768]{1,0:T(8,128)(2,1)S(1)} %get-tuple-element.630), channel_id=1, replica_groups=mesh['seq'=8,'tp'=4] {'tp'}, dimensions={0}, use_global_device_ids=true | all-gather | bytes 983040 | tf_op jit(solution)/shard_map/all_gather | solution.py:215
  41.7 3.2 fusion.121
  45.0 48.1 %all-gather.7.cloned.1.call-done = bf16[4096,768]{1,0:T(8,128)(2,1)} async-done(((bf16[128,768]{1,0:T(8,128)(2,1)}), bf16[4096,768]{1,0:T(8,128)(2,1)}) %all-gather.7.cloned.1.call-update) | async-done | bytes 6291472 | tf_op jit(solution)/shard_map/all_gather | solution.py:187
  93.0 8.6 copy.39
  101.6 72.4 %all-gather.5.cloned.1.call-done = bf16[4096,768]{0,1:T(8,128)(2,1)} async-done(((bf16[128,768]{0,1:T(8,128)(2,1)}), bf16[4096,768]{0,1:T(8,128)(2,1)}) %all-gather.5.cloned.1.call-update) | async-done | bytes 6291472 | tf_op jit(solution)/shard_map/all_gather | solution.py:186
  174.1 46.2 %while.48 = (s32[]{:T(128)}, f32[12,128]{1,0:T(8,128)S(1)}, f32[12,128]{1,0:T(8,128)}, f32[128,12,64]{0,2,1:T(8,128)}, bf16[4096,768]{0,1:T(8,128)(2,1)}, /*inde...) while((s32[]{:T(128)}, f32[12,128]{1,0:T(8,128)S(1)}, ...), condition=%wide.region_5.6_spmd.clone, body=%wide.region_2.5_spmd.clone.sunk | while | flops 830776320 | bytes 108871960 | solution.py:65
  174.1 5.4 constant_dynamic-slice_fusion.6
  179.5 5.7 bitcast_reduce_fusion.2
  185.2 8.8 fusion.179
  194.5 2.0 fusion.177
  197.1 5.4 constant_dynamic-slice_fusion.6
  202.5 5.7 bitcast_reduce_fusion.2
  208.2 8.8 fusion.179
  217.6 2.0 fusion.177
  221.5 2.6 fusion.117
  225.0 8.9 %all_gather.28 = bf16[512,768]{1,0:T(8,128)(2,1)S(1)} all-gather(bf16[128,768]{1,0:T(8,128)(2,1)S(1)} %add_convert_fusion.4), channel_id=1, replica_groups=mesh['seq'=8,'tp'=4] {'tp'}, dimensions={0}, use_global_device_ids=true | all-gather | bytes 983040 | tf_op jit(solution)/shard_map/all_gather | solution.py:199
  233.9 3.4 convert_reduce_fusion
  238.2 1.7 convolution_convert_fusion
  240.0 3.7 convolution_convert_fusion.1
  245.6 15.9 %reduce-scatter.5.cloned.1.call-done = bf16[128,768]{1,0:T(8,128)(2,1)} async-done(((bf16[512,768]{1,0:T(8,128)(2,1)}), bf16[128,768]{1,0:T(8,128)(2,1)}) %reduce-scatter.5.cloned.1.call-update) | async-done | bytes 196624 | tf_op jit(solution)/shard_map/reduce_scatter | solution.py:222
  263.9 2.0 fusion.89
  266.4 21.5 %reduce-scatter.3.cloned.1.call-done = bf16[128,768]{1,0:T(8,128)(2,1)} async-done(((bf16[512,768]{1,0:T(8,128)(2,1)}), bf16[128,768]{1,0:T(8,128)(2,1)}) %reduce-scatter.3.cloned.1.call-update) | async-done | bytes 196624 | tf_op jit(solution)/shard_map/reduce_scatter | solution.py:204
  288.0 3.0 multiply_reduce_fusion
  291.8 1.9 convolution_convert_fusion.2
  293.7 1.7 copy.40
  295.5 2.1 copy.41
  297.6 1.7 copy.44
  299.4 2.1 copy.45
  302.1 44.5 %all_gather.31 = f32[4096,12]{0,1:T(8,128)} all-gather(f32[128,12]{0,1:T(8,128)S(1)} %bitcast.159), channel_id=1, replica_groups=mesh['seq'=8,'tp'=4] {'seq','tp'}, dimensions={0}, use_global_device_ids=true | all-gather | bytes 202752 | tf_op jit(solution)/shard_map/all_gather | solution.py:265
  346.6 3.7 fusion.122
  350.3 2.3 fusion.113
  352.8 1.8 multiply_reduce_fusion.5
  354.5 2.1 copy.43
  356.7 3.0 fusion.100
  359.6 40.3 %all_gather.33 = f32[4096,12]{0,1:T(8,128)} all-gather(f32[128,12]{0,1:T(8,128)S(1)} %copy-done.45), channel_id=1, replica_groups=mesh['seq'=8,'tp'=4] {'seq','tp'}, dimensions={0}, use_global_device_ids=true | all-gather | bytes 202752 | tf_op jit(solution)/shard_map/all_gather | solution.py:266
  400.0 46.7 %while.49 = (s32[]{:T(128)}, f32[128,12,64]{0,2,1:T(8,128)}, bf16[4096,768]{0,1:T(8,128)(2,1)}, bf16[128,12,64]{2,1,0:T(8,128)(2,1)}, f32[12,128]{1,0:T(8,128)},...) while((s32[]{:T(128)}, f32[128,12,64]{0,2,1:T(8,128)}, ...), condition=%wide.region_14.15_spmd.clone, body=%wide.region_13.14_spmd.clone.sunk | while | flops 1223983104 | bytes 61747432 | solution.py:65
  400.0 5.4 constant_dynamic-slice_fusion.7
  405.4 5.7 fusion.185
  411.1 12.3 %fusion.186 = f32[128,12,64]{0,2,1:T(8,128)} fusion(bf16[2048,12,64]{0,2,1:T(8,128)(2,1)} %bitcast.140, f32[12,2048,128]{2,1,0:T(8,128)} %fusion.185, f32[12,128]{1,0:T(8,128)S(1)} %get-tuple-element.950, f32[12,128]{1,0:T(8,128)} %get-tuple-element.947, bf16[2048,12,64]{0,2,1:T(8,128)(2,1)} %bitcast.141, ...), kind=kOutput, calls=%fused_computation.24.clone.1 | convolution fusion | flops 821329920 | bytes 19869696 | tf_op jit(solution)/shard_map/while/body/eval_jaxpr/hqk,khd->qhd/dot_general | solution.py:99
  423.4 5.5 constant_dynamic-slice_fusion.7
  428.9 5.7 fusion.185
  434.5 12.2 %fusion.186 = f32[128,12,64]{0,2,1:T(8,128)} fusion(bf16[2048,12,64]{0,2,1:T(8,128)(2,1)} %bitcast.140, f32[12,2048,128]{2,1,0:T(8,128)} %fusion.185, f32[12,128]{1,0:T(8,128)S(1)} %get-tuple-element.950, f32[12,128]{1,0:T(8,128)} %get-tuple-element.947, bf16[2048,12,64]{0,2,1:T(8,128)(2,1)} %bitcast.141, ...), kind=kOutput, calls=%fused_computation.24.clone.1 | convolution fusion | flops 821329920 | bytes 19869696 | tf_op jit(solution)/shard_map/while/body/eval_jaxpr/hqk,khd->qhd/dot_general | solution.py:99
  446.7 4.3 all-gather.11.cloned.1.call-done
  451.0 71.5 %while.50 = (s32[]{:T(128)}, f32[128,12,64]{0,2,1:T(8,128)}, f32[128,12,64]{0,2,1:T(8,128)}, bf16[4096,12,64]{0,2,1:T(8,128)(2,1)}, bf16[128,12,64]{0,2,1:T(8,12...) while((s32[]{:T(128)}, f32[128,12,64]{0,2,1:T(8,128)}, ...), condition=%wide.region_16.17_spmd.clone, body=%wide.region_15.16_spmd.clone.sunk | while | flops 1636270080 | bytes 54986488 | solution.py:65
  459.9 8.5 fusion.194
  469.1 8.4 fusion.196
  477.6 13.6 %fusion.195 = f32[128,12,64]{0,2,1:T(8,128)} fusion(f32[12,2048,128]{2,1,0:T(8,128)} %fusion.194, f32[12,2048]{1,0:T(8,128)} %get-tuple-element.845, f32[12,2048]{1,0:T(8,128)} %get-tuple-element.846, bf16[4096,12,64]{0,2,1:T(8,128)(2,1)} %get-tuple-element.912, s32[]{:T(128)S(6)} %select_n.34, bf16[4096,12,64]{0,2,1:T(8,128)(2,1)} %get-tuple-element.909, ...), kind=kOutput, calls=%fused_computation.48.clone.1 | convolution fusion | flops 821329920 | bytes 20448768 | tf_op jit(solution)/shard_map/while/body/eval_jaxpr/hqk,qhd->khd/dot_general | solution.py:120
  491.2 8.4 fusion.194
  500.3 8.5 fusion.196
  508.8 13.7 %fusion.195 = f32[128,12,64]{0,2,1:T(8,128)} fusion(f32[12,2048,128]{2,1,0:T(8,128)} %fusion.194, f32[12,2048]{1,0:T(8,128)} %get-tuple-element.845, f32[12,2048]{1,0:T(8,128)} %get-tuple-element.846, bf16[4096,12,64]{0,2,1:T(8,128)(2,1)} %get-tuple-element.912, s32[]{:T(128)S(6)} %select_n.34, bf16[4096,12,64]{0,2,1:T(8,128)(2,1)} %get-tuple-element.909, ...), kind=kOutput, calls=%fused_computation.48.clone.1 | convolution fusion | flops 821329920 | bytes 20448768 | tf_op jit(solution)/shard_map/while/body/eval_jaxpr/hqk,qhd->khd/dot_general | solution.py:120
  525.3 2.7 multiply_reduce_fusion.1
  528.2 4.2 fusion.97
  532.5 1.7 broadcast_multiply_fusion
  534.2 19.7 %psum.85 = f32[768]{0:T(1024)} all-reduce(f32[768]{0:T(1024)} %get-tuple-element.627), channel_id=1, replica_groups=mesh['seq'=8,'tp'=4] {'seq'}, use_global_device_ids=true, to_apply=%region_37.38 | all-reduce | flops 768 | bytes 6144 | tf_op jit(solution)/shard_map/psum | solution.py:327
  555.9 1.9 multiply_reduce_fusion.3
  557.8 42.9 %all-reduce.4 = (f32[768]{0:T(1024)}, f32[768]{0:T(1024)}, f32[768]{0:T(1024)}, f32[4608]{0:T(1024)}, f32[768]{0:T(1024)}) all-reduce(f32[768]{0:T(1024)S(1)} %get-tuple-element.633, f32[768]{0:T(1024)} %get-tuple-element.561, f32[768]{0:T(1024)} %get-tuple-element.564, ...), channel_id=1, replica_groups=mesh['seq'=8,'tp'=4] {'seq','tp'}, use_global_device_ids=true, to_apply=%region_20.21 | all-reduce | flops 7680 | bytes 61440 | tf_op jit(solution)/shard_map/psum | solution.py:314
  600.7 24.5 %all-reduce.12.cloned.1.call-done = (f32[768,768]{1,0:T(8,128)}, f32[768,768]{1,0:T(8,128)}) async-done(((f32[768,768]{1,0:T(8,128)}, f32[768,768]{1,0:T(8,128)}), (f32[768,768]{1,0:T(8,128)}, f32[768,768]{1,0:T(8,128)})) %all-reduce.12.cloned.1.call-update) | async-done | bytes 4718608 | tf_op jit(solution)/shard_map/psum | solution.py:327
  625.1 231.1 %all-reduce.10.cloned.1.call-done = (f32[128,4608]{1,0:T(8,128)}, f32[768,2304]{1,0:T(8,128)}, f32[768,768]{1,0:T(8,128)}) async-done(((f32[128,4608]{1,0:T(8,128)}, f32[768,2304]{1,0:T(8,128)}, f32[768,768]{1,0:T(8,128)}), (f32[128,4608]{1,0:T(8,128)}, f32[768,2304]{1,0:T(8,128)}, f32[768,768]{1,0:T(8,128)})) %all-reduce.10.cloned.1.call-update) | async-done | bytes 11796496 | tf_op jit(solution)/shard_map/psum | solution.py:314
  856.2 3.2 copy.104
  859.5 6.6 copy.105
  (234 shorter events, 38.2 us)
Async XLA Ops:
  7.2 9.4 %copy-start = (bf16[768,2304]{1,0:T(8,128)(2,1)S(1)}, bf16[768,2304]{1,0:T(8,128)(2,1)}, u32[]{:S(2)}) copy-start(bf16[768,2304]{1,0:T(8,128)(2,1)} %param.32) | copy-start | bytes 10616836
  7.2 85.8 %all-gather.7.cloned.1.call-start = ((), (), s32[]{:S(2)}) async-start(), calls=%async_computation.3 | async-start | bytes 6488064 | tf_op jit(solution)/shard_map/all_gather | solution.py:187
  8.9 9.3 %copy-start.28 = (f32[768]{0:T(1024)}, f32[768]{0:T(1024)S(1)}, u32[]{:S(2)}) copy-start(f32[768]{0:T(1024)S(1)} %convert_element_type.131) | copy-start | bytes 9220
  9.6 8.7 copy-start.42
  10.7 7.6 copy-start.52
  11.9 6.4 copy-start.55
  12.7 3.9 copy-start.61
  15.9 2.4 copy-start.31
  15.9 2.4 copy-start.35
  15.9 12.2 %copy-start.44 = (f32[768]{0:T(1024)}, f32[768]{0:T(1024)S(1)}, u32[]{:S(2)}) copy-start(f32[768]{0:T(1024)S(1)} %get-tuple-element.667) | copy-start | bytes 9220
  16.6 1.7 copy-start.33
  20.1 154.0 %all-gather.5.cloned.1.call-start = ((), (), s32[]{:S(2)}) async-start(), calls=%async_computation.2 | async-start | bytes 6488064 | tf_op jit(solution)/shard_map/all_gather | solution.py:186
  22.8 1.7 copy-start.7
  23.0 2.4 copy-start.30
  23.0 2.4 copy-start.23
  24.4 1.8 copy-start.60
  26.1 235.4 %reduce-scatter.5.cloned.1.call-start = ((), (), s32[]{:S(2)}) async-start(), calls=%async_computation.5 | async-start | bytes 983040 | tf_op jit(solution)/shard_map/reduce_scatter | solution.py:222
  174.1 5.4 copy-start.4
  185.2 9.2 %copy-start.1 = (f32[12,2048,128]{2,1,0:T(8,128)S(1)}, f32[12,2048,128]{2,1,0:T(8,128)}, u32[]{:S(2)}) copy-start(f32[12,2048,128]{2,1,0:T(8,128)} %get-tuple-element.823) | copy-start | bytes 37748740 | tf_op jit(solution)/shard_map/while
  194.5 2.0 copy-start.25
  197.1 5.4 copy-start.4
  208.2 9.4 %copy-start.1 = (f32[12,2048,128]{2,1,0:T(8,128)S(1)}, f32[12,2048,128]{2,1,0:T(8,128)}, u32[]{:S(2)}) copy-start(f32[12,2048,128]{2,1,0:T(8,128)} %get-tuple-element.823) | copy-start | bytes 37748740 | tf_op jit(solution)/shard_map/while
  217.6 2.0 copy-start.25
  220.3 4.6 copy-start.37
  220.3 4.6 copy-start.38
  220.3 4.6 copy-start.47
  220.3 13.6 %copy-start.58 = (f32[768]{0:T(1024)S(1)}, f32[768]{0:T(1024)}, u32[]{:S(2)}) copy-start(f32[768]{0:T(1024)} %convert_element_type.144) | copy-start | bytes 9220
  220.3 13.6 %copy-start.65 = (bf16[768,768]{1,0:T(8,128)(2,1)S(1)}, bf16[768,768]{1,0:T(8,128)(2,1)}, u32[]{:S(2)}) copy-start(bf16[768,768]{1,0:T(8,128)(2,1)} %param.34) | copy-start | bytes 3538948
  220.3 13.6 %copy-start.66 = (f32[512,768]{1,0:T(8,128)S(1)}, f32[512,768]{1,0:T(8,128)}, u32[]{:S(2)}) copy-start(f32[512,768]{1,0:T(8,128)} %fusion.121) | copy-start | bytes 4718596
  221.5 3.5 copy-start.17
  233.9 3.4 copy-start.9
  239.9 48.0 %reduce-scatter.3.cloned.1.call-start = ((), (), s32[]{:S(2)}) async-start(), calls=%async_computation.4 | async-start | bytes 983040 | tf_op jit(solution)/shard_map/reduce_scatter | solution.py:204
  243.7 203.0 %all-gather.9.cloned.1.call-start = ((), (), s32[]{:S(2)}) async-start(), calls=%async_computation.6 | async-start | bytes 6488064 | tf_op jit(solution)/shard_map/all_gather | solution.py:283
  244.3 206.7 %all-gather.11.cloned.1.call-start = ((), (), s32[]{:S(2)}) async-start(), calls=%async_computation.7 | async-start | bytes 6488064 | tf_op jit(solution)/shard_map/all_gather | solution.py:284
  288.0 3.8 copy-start.11
  291.0 10.5 %copy-start.27 = (f32[12,128]{1,0:T(8,128)S(1)}, f32[12,128]{1,0:T(8,128)}, u32[]{:S(2)}) copy-start(f32[12,128]{1,0:T(8,128)} %get-tuple-element.434) | copy-start | bytes 18436
  295.4 329.7 %all-reduce.12.cloned.1.call-start = ((), (), s32[]{:S(2)}) async-start(), calls=%async_computation.9 | async-start | bytes 9437184 | tf_op jit(solution)/shard_map/psum | solution.py:327
  346.6 3.7 copy-start.21
  346.6 3.7 copy-start.67
  352.7 4.0 copy-start.41
  352.7 503.5 %all-reduce.10.cloned.1.call-start = ((), (), s32[]{:S(2)}) async-start(), calls=%async_computation.8 | async-start | bytes 23592960 | tf_op jit(solution)/shard_map/psum | solution.py:314
  354.5 5.1 copy-start.45
  400.0 5.4 copy-start.5
  405.4 5.7 copy-start.2
  423.4 5.5 copy-start.5
  428.9 5.7 copy-start.2
  459.9 8.6 copy-start.12
  459.9 8.5 copy-start.13
  491.2 8.4 copy-start.12
  491.2 8.4 copy-start.13
  522.5 2.5 copy-start.18
  522.5 2.5 copy-start.19
  522.5 2.6 copy-start.24
  525.3 2.8 copy-start.39
  525.3 2.8 copy-start.51
  525.3 2.8 copy-start.49
  525.3 2.8 copy-start.48
  525.3 2.8 copy-start.50
  525.3 2.8 copy-start.36
  528.2 4.3 copy-start.40
  528.2 4.3 copy-start.62
  859.5 6.6 copy-start.16
  866.1 2.5 copy-start.15
  868.6 2.5 copy-start.14
  (20 other events, 20.6 us)
Sparse Core Ops, SparseCore 0:
  20.2 72.7 all-gather.6
  96.4 77.5 all-gather.4
  240.0 21.4 reduce-scatter.4
  264.7 23.2 reduce-scatter.2
  290.6 80.2 all-gather.8
  373.6 77.3 all-gather.10
  455.7 169.3 all-reduce.11
  632.7 223.5 all-reduce.9
where the time goes:
time: 894 us; the launch traced here: 880 us
  waiting for transfers between devices  418 us (47%)
  blocking collectives  167 us (19%)
  matrix products  162 us (18%)
  local copies, waits for them, and re-layouts  70.2 us (8%)
  other arithmetic  35.6 us (4%)
  between operations  16.5 us (2%)
  loops' own time  9.02 us (1%)
    psum x1, waiting for transfers between devices, per_device(): lax.psum((qkv_weight_grad, out_weight_grad, ada_weight_grad, modulation_g...  231 us
    all_gather x1, waiting for transfers between devices, per_device(): lax.all_gather(key_rows, ('seq', 'tp'), axis=0, tiled=True)  72.4 us
    all_gather x1, waiting for transfers between devices, per_device(): lax.all_gather(value_rows, ('seq', 'tp'), axis=0, tiled=True)  48.1 us
    all_gather x1, blocking collectives, per_device(): lax.all_gather(logsum.T, ('seq', 'tp'), axis=0, tiled=True)  44.5 us
    psum x1, blocking collectives, per_device(): lax.psum((qkv_weight_grad, out_weight_grad, ada_weight_grad, modulation_g...  42.9 us
    all_gather x1, blocking collectives, per_device(): lax.all_gather(delta_rows, ('seq', 'tp'), axis=0, tiled=True)  40.3 us
    unnamed x134, local copies, waits for them, and re-layouts  36.7 us
    dot_general x2, matrix products, key_update(): jnp.einsum('hqk,qhd->khd', score_grad, query_block, preferred_element_typ...  27.2 us
  transfers between devices with their start and end apart: 8, of which 7 were waited for; matrix products, arithmetic and copies ran while one was open for 21% of the time, Pallas kernels for 0%

commit v1 on v0

--- a/solution.py
+++ b/solution.py
@@ -121,6 +121,14 @@
         "hqk,qhd->khd", score_grad, query_block, preferred_element_type=jnp.float32
     )
     return (key_grad, value_grad)
+
+
+def to_heads(rows):
+    return lax.all_to_all(rows, "tp", split_axis=1, concat_axis=0, tiled=True)
+
+
+def to_rows(rows):
+    return lax.all_to_all(rows, "tp", split_axis=0, concat_axis=1, tiled=True)
 
 
 def per_device(
@@ -160,39 +168,44 @@
     normed = modulate(start, gain_one, shift_one, scale_one).astype(jnp.bfloat16)
     projected = jnp.dot(normed, qkv_weight, preferred_element_type=jnp.float32)
     split_rows = projected.reshape(row_count, 3, head_count, head_width)
-    queries = rotate(split_rows[:, 0], cosine, sine).astype(jnp.bfloat16)
-    key_rows = (
-        rotate(split_rows[:, 1], cosine, sine).reshape(row_count, model_width).astype(jnp.bfloat16)
-    )
-    value_rows = projected[:, 2 * model_width :].astype(jnp.bfloat16)
+    queries, key_rows, value_rows = (
+        to_heads(rows.reshape(row_count, model_width).astype(jnp.bfloat16))
+        for rows in (
+            rotate(split_rows[:, 0], cosine, sine),
+            rotate(split_rows[:, 1], cosine, sine),
+            split_rows[:, 2],
+        )
+    )
+    group_size, group_width = queries.shape
+    head_group = group_width // head_width
+    queries = queries.reshape(group_size, head_group, head_width)
+    every_key = lax.all_gather(key_rows, "seq", axis=0, tiled=True)
+    every_value = lax.all_gather(value_rows, "seq", axis=0, tiled=True)
     initial = (
-        jnp.full((head_count, row_count), floor_value, jnp.float32),
-        jnp.zeros((head_count, row_count), jnp.float32),
-        jnp.zeros((row_count, head_count, head_width), jnp.float32),
+        jnp.full((head_group, group_size), floor_value, jnp.float32),
+        jnp.zeros((head_group, group_size), jnp.float32),
+        jnp.zeros((group_size, head_group, head_width), jnp.float32),
     )
 
     def advance(current, blocks):
         return forward_update(
             current,
             queries,
-            blocks[0].reshape(-1, head_count, head_width),
-            blocks[1].reshape(-1, head_count, head_width),
+            blocks[0].reshape(-1, head_group, head_width),
+            blocks[1].reshape(-1, head_group, head_width),
             score_scale,
         )
 
     running = over_blocks(
         initial,
-        (
-            lax.all_gather(key_rows, ("seq", "tp"), axis=0, tiled=True),
-            lax.all_gather(value_rows, ("seq", "tp"), axis=0, tiled=True),
-        ),
-        row_count,
+        (every_key, every_value),
+        group_size,
         advance,
     )
     highest_seen, totals, weighted = running
     logsum = highest_seen + jnp.log(totals)
     attended = weighted / totals.T[:, :, None]
-    mixed = attended.reshape(row_count, model_width).astype(jnp.bfloat16)
+    mixed = to_rows(attended.reshape(group_size, group_width).astype(jnp.bfloat16))
     branch = jnp.dot(mixed, out_weight, preferred_element_type=jnp.float32)
     middle = start + gate_one * branch
     normed_two = modulate(middle, gain_two, shift_two, scale_two).astype(jnp.bfloat16)
@@ -231,14 +244,12 @@
     gate_one_grad = jnp.sum(middle_grad * branch, axis=0)
     branch_grad = (middle_grad * gate_one).astype(jnp.bfloat16)
     out_weight_grad = jnp.dot(mixed.T, branch_grad, preferred_element_type=jnp.float32)
-    mixed_grad = (
-        jnp.dot(branch_grad, out_weight.T, preferred_element_type=jnp.float32)
-        .astype(jnp.bfloat16)
-        .reshape(row_count, head_count, head_width)
-    )
+    mixed_grad = to_heads(
+        jnp.dot(branch_grad, out_weight.T, preferred_element_type=jnp.float32).astype(jnp.bfloat16)
+    ).reshape(group_size, head_group, head_width)
     delta_rows = jnp.sum(mixed_grad.astype(jnp.float32) * attended, axis=-1)
     delta = delta_rows.T
-    initial_query = jnp.zeros((row_count, head_count, head_width), jnp.float32)
+    initial_query = jnp.zeros((group_size, head_group, head_width), jnp.float32)
 
     def advance(grads_now, blocks):
         return query_update(
@@ -247,52 +258,60 @@
             mixed_grad,
             logsum,
             delta,
-            blocks[0].reshape(-1, head_count, head_width),
-            blocks[1].reshape(-1, head_count, head_width),
+            blocks[0].reshape(-1, head_group, head_width),
+            blocks[1].reshape(-1, head_group, head_width),
             score_scale,
         )
 
     query_grad = over_blocks(
         initial_query,
-        (
-            lax.all_gather(key_rows, ("seq", "tp"), axis=0, tiled=True),
-            lax.all_gather(value_rows, ("seq", "tp"), axis=0, tiled=True),
-        ),
-        row_count,
+        (every_key, every_value),
+        group_size,
         advance,
     )
     every_logsum, every_delta = (
-        lax.all_gather(logsum.T, ("seq", "tp"), axis=0, tiled=True),
-        lax.all_gather(delta_rows, ("seq", "tp"), axis=0, tiled=True),
-    )
-    own_keys = key_rows.reshape(row_count, head_count, head_width)
-    own_values = value_rows.reshape(row_count, head_count, head_width)
+        lax.all_gather(logsum.T, "seq", axis=0, tiled=True),
+        lax.all_gather(delta_rows, "seq", axis=0, tiled=True),
+    )
+    own_keys = key_rows.reshape(group_size, head_group, head_width)
+    own_values = value_rows.reshape(group_size, head_group, head_width)
     initial_keys = (
-        jnp.zeros((row_count, head_count, head_width), jnp.float32),
-        jnp.zeros((row_count, head_count, head_width), jnp.float32),
+        jnp.zeros((group_size, head_group, head_width), jnp.float32),
+        jnp.zeros((group_size, head_group, head_width), jnp.float32),
     )
 
     def advance(grads_now, blocks):
         return key_update(
-            grads_now, blocks[0], blocks[1], blocks[2], blocks[3], own_keys, own_values, score_scale
+            grads_now,
+            blocks[0].reshape(-1, head_group, head_width),
+            blocks[1].reshape(-1, head_group, head_width),
+            blocks[2],
+            blocks[3],
+            own_keys,
+            own_values,
+            score_scale,
         )
 
     key_grad, value_grad = over_blocks(
         initial_keys,
         (
-            lax.all_gather(queries, ("seq", "tp"), axis=0, tiled=True),
-            lax.all_gather(mixed_grad, ("seq", "tp"), axis=0, tiled=True),
+            lax.all_gather(queries.reshape(group_size, group_width), "seq", axis=0, tiled=True),
+            lax.all_gather(mixed_grad.reshape(group_size, group_width), "seq", axis=0, tiled=True),
             every_logsum,
             every_delta,
         ),
-        row_count,
+        group_size,
         advance,
     )
-    unused, rotate_back = jax.vjp(lambda head_rows: rotate(head_rows, cosine, sine), query_grad)
-    query_part = rotate_back(query_grad)[0].reshape(row_count, model_width)
-    key_part = rotate_back(key_grad)[0].reshape(row_count, model_width)
+    query_rows, key_part_rows, value_grad_rows = (
+        to_rows(rows.reshape(group_size, group_width)).reshape(row_count, head_count, head_width)
+        for rows in (query_grad, key_grad, value_grad)
+    )
+    unused, rotate_back = jax.vjp(lambda head_rows: rotate(head_rows, cosine, sine), query_rows)
+    query_part = rotate_back(query_rows)[0].reshape(row_count, model_width)
+    key_part = rotate_back(key_part_rows)[0].reshape(row_count, model_width)
     projected_grad = jnp.concatenate(
-        [query_part, key_part, value_grad.reshape(row_count, model_width)], axis=1
+        [query_part, key_part, value_grad_rows.reshape(row_count, model_width)], axis=1
     ).astype(jnp.bfloat16)
     qkv_weight_grad = jnp.dot(normed.T, projected_grad, preferred_element_type=jnp.float32)
     normed_grad = jnp.dot(projected_grad, qkv_weight.T, preferred_element_type=jnp.float32)
@@ -310,12 +329,10 @@
             gate_two_grad,
         ]
     )
-    ada_weight_grad = activation[:, None] * modulation_grad[None, :]
     summed = lax.psum(
         (
             qkv_weight_grad,
             out_weight_grad,
-            ada_weight_grad,
             modulation_grad,
             gain_one_grad,
             gain_two_grad,
@@ -328,17 +345,17 @@
     return (
         output,
         start_grad,
-        summed[7],
+        summed[6],
+        summed[3],
         summed[4],
-        summed[5],
+        activation[:, None] * summed[2][None, :],
         summed[2],
-        summed[3],
         summed[0],
         summed[1],
         split_sums[0],
         split_sums[1],
         split_sums[2],
-        summed[6],
+        summed[5],
     )
 
 

time: 894 us -> 743 us (0.83)
  waiting for transfers between devices: 418 us -> 259 us
  starting transfers between devices: 0.33 us -> 30.1 us
  matrix products: 162 us -> 147 us
    psum x1, waiting for transfers between devices: 231 us -> 156 us  [per_device(): lax.psum((qkv_weight_grad, out_weight_grad, modulation_grad, gain_one_gra...]
    all_gather x4, waiting for transfers between devices: 125 us -> 63.2 us  [the longest x1 46.1 us: per_device(): every_value = lax.all_gather(value_rows, 'seq', axis=0, tiled=True)]
    all_to_all x0 -> x5, starting transfers between devices: none -> 29.5 us  [the longest x4 25.5 us: to_rows(): return lax.all_to_all(rows, 'tp', split_axis=0, concat_axis=1, tiled=True)]
    all_to_all x0 -> x3, blocking collectives: none -> 25.7 us  [to_heads(): return lax.all_to_all(rows, 'tp', split_axis=1, concat_axis=0, tiled=True)]
    psum x1, waiting for transfers between devices: 24.5 us -> 0.01 us  [per_device(): lax.psum((up_weight_grad, up_bias_grad, down_weight_grad), 'seq')]
    all_to_all x0 -> x14, local copies, waits for them, and re-layouts: none -> 21.5 us  [the longest x8 10.7 us: to_heads(): return lax.all_to_all(rows, 'tp', split_axis=1, concat_axis=0, tiled=True)]
    all_gather x2, blocking collectives: 84.8 us -> 65 us  [the longest x1 32.6 us: per_device(): lax.all_gather(delta_rows, 'seq', axis=0, tiled=True)]
    unnamed x134 -> x141, local copies, waits for them, and re-layouts: 36.7 us -> 20.5 us
  transfers between devices with their start and end apart: 8 -> 13, of which waited for: 7 -> 8; matrix products, arithmetic and copies ran while one was open for 21% -> 22% of each run, Pallas kernels for 0% -> 0%
where the time goes in v1:
time: 743 us; the launch traced here: 729 us
  waiting for transfers between devices  259 us (35%)
  blocking collectives  171 us (23%)
  matrix products  147 us (20%)
  local copies, waits for them, and re-layouts  73.6 us (10%)
  other arithmetic  31.7 us (4%)
  starting transfers between devices  30.1 us (4%)
  between operations  16.5 us (2%)
    psum x1, waiting for transfers between devices, per_device(): lax.psum((qkv_weight_grad, out_weight_grad, modulation_grad, gain_one_gra...  156 us
    all_gather x1, waiting for transfers between devices, per_device(): every_value = lax.all_gather(value_rows, 'seq', axis=0, tiled=True)  46.1 us
    psum x1, blocking collectives, per_device(): lax.psum((qkv_weight_grad, out_weight_grad, modulation_grad, gain_one_gra...  39.8 us
    all_gather x1, blocking collectives, per_device(): lax.all_gather(delta_rows, 'seq', axis=0, tiled=True)  32.6 us
    all_gather x1, blocking collectives, per_device(): lax.all_gather(logsum.T, 'seq', axis=0, tiled=True)  32.4 us
    all_to_all x3, blocking collectives, to_heads(): return lax.all_to_all(rows, 'tp', split_axis=1, concat_axis=0, tiled=True)  25.7 us
    all_to_all x4, starting transfers between devices, to_rows(): return lax.all_to_all(rows, 'tp', split_axis=0, concat_axis=1, tiled=True)  25.5 us
    psum x1, blocking collectives, per_device(): lax.psum((up_weight_grad, up_bias_grad, down_weight_grad), 'seq')  22.6 us
  transfers between devices with their start and end apart: 13, of which 8 were waited for; matrix products, arithmetic and copies ran while one was open for 22% of the time, Pallas kernels for 0%

profile of v1, /device:TPU:0, one launch (start us, length us, event | category | flops | bytes accessed | tf_op | source)
XLA Modules:
  0.0 728.8 jit_solution(12411963143510230814)
XLA Ops:
  13.6 1.8 convolution_reduce_fusion
  20.4 9.4 %all_to_all.136 = bf16[128,4,192]{0,2,1:T(8,128)(2,1)S(1)} all-to-all(bf16[128,4,192]{0,2,1:T(8,128)(2,1)S(1)} %get-tuple-element.644), channel_id=1, replica_groups=mesh['seq'=8,'tp'=4] {'tp'}, dimensions={1} | all-to-all | bytes 393216 | tf_op jit(solution)/shard_map/all_to_all | solution.py:127
  32.3 7.7 %all_to_all.137 = bf16[128,4,192]{0,2,1:T(8,128)(2,1)S(1)} all-to-all(bf16[128,4,192]{0,2,1:T(8,128)(2,1)S(1)} %bitcast.239), channel_id=1, replica_groups=mesh['seq'=8,'tp'=4] {'tp'}, dimensions={1} | all-to-all | bytes 393216 | tf_op jit(solution)/shard_map/all_to_all | solution.py:127
  41.4 4.0 all-to-all-start.1
  47.0 9.5 %all_gather.27 = bf16[512,768]{1,0:T(8,128)(2,1)} all-gather(bf16[128,768]{1,0:T(8,128)(2,1)S(1)} %get-tuple-element.614), channel_id=1, replica_groups=mesh['seq'=8,'tp'=4] {'tp'}, dimensions={0}, use_global_device_ids=true | all-gather | bytes 983040 | tf_op jit(solution)/shard_map/all_gather | solution.py:228
  60.0 17.0 %all-gather.5.cloned.1.call-done = bf16[4096,192]{0,1:T(8,128)(2,1)} async-done(((bf16[512,192]{0,1:T(8,128)(2,1)}), bf16[4096,192]{0,1:T(8,128)(2,1)}) %all-gather.5.cloned.1.call-update) | async-done | bytes 1572880 | tf_op jit(solution)/shard_map/all_gather | solution.py:182
  77.0 46.1 %all-gather.7.cloned.1.call-done = bf16[4096,192]{0,1:T(8,128)(2,1)} async-done(((bf16[512,192]{0,1:T(8,128)(2,1)}), bf16[4096,192]{0,1:T(8,128)(2,1)}) %all-gather.7.cloned.1.call-update) | async-done | bytes 1572880 | tf_op jit(solution)/shard_map/all_gather | solution.py:183
  123.1 40.3 %while.48 = (s32[]{:T(128)}, f32[3,512]{1,0:T(4,128)S(1)}, f32[3,512]{1,0:T(4,128)}, f32[512,3,64]{0,2,1:T(8,128)}, bf16[4096,192]{0,1:T(8,128)(2,1)}, /*index=5...) while((s32[]{:T(128)}, f32[3,512]{1,0:T(4,128)S(1)}, ...), condition=%wide.region_5.6_spmd.clone, body=%wide.region_2.5_spmd.clone.sunk | while | flops 830776320 | bytes 94716184 | solution.py:65
  123.1 2.4 constant_dynamic-slice_fusion.9
  125.5 6.4 bitcast_reduce_fusion.2
  132.0 7.9 %fusion.157 = f32[512,3,64]{0,2,1:T(8,128)} fusion(bf16[2048,3,64]{0,2,1:T(8,128)(2,1)} %bitcast.227, f32[3,2048,512]{2,1,0:T(8,128)} %get-tuple-element.813, f32[3,512]{1,0:T(4,128)S(1)} %get-tuple-element.862, f32[512,3,64]{0,2,1:T(8,128)} %get-tuple-element.853, f32[512,3]{0,1:T(4,128)S(1)} %get-tuple-element.815, pred[]{:T(512)S(6)} %compare.13), kind=kOutput, calls=%fused_computation.7.clone.1 | convolution fusion | flops 412385280 | bytes 14168065 | tf_op jit(solution)/shard_map/while/body/eval_jaxpr/hqk,khd->qhd/dot_general | solution.py:78
  140.5 2.0 fusion.155
  143.2 2.4 constant_dynamic-slice_fusion.9
  145.6 6.4 bitcast_reduce_fusion.2
  152.0 7.9 %fusion.157 = f32[512,3,64]{0,2,1:T(8,128)} fusion(bf16[2048,3,64]{0,2,1:T(8,128)(2,1)} %bitcast.227, f32[3,2048,512]{2,1,0:T(8,128)} %get-tuple-element.813, f32[3,512]{1,0:T(4,128)S(1)} %get-tuple-element.862, f32[512,3,64]{0,2,1:T(8,128)} %get-tuple-element.853, f32[512,3]{0,1:T(4,128)S(1)} %get-tuple-element.815, pred[]{:T(512)S(6)} %compare.13), kind=kOutput, calls=%fused_computation.7.clone.1 | convolution fusion | flops 412385280 | bytes 14168065 | tf_op jit(solution)/shard_map/while/body/eval_jaxpr/hqk,khd->qhd/dot_general | solution.py:78
  160.7 2.0 fusion.155
  168.3 4.0 all-to-all-start.3
  172.7 3.5 fusion.88
  177.7 2.6 fusion.82
  181.3 8.7 %all_gather.26 = bf16[512,768]{1,0:T(8,128)(2,1)S(1)} all-gather(bf16[128,768]{1,0:T(8,128)(2,1)S(1)} %add_convert_fusion.3), channel_id=1, replica_groups=mesh['seq'=8,'tp'=4] {'tp'}, dimensions={0}, use_global_device_ids=true | all-gather | bytes 983040 | tf_op jit(solution)/shard_map/all_gather | solution.py:212
  190.0 3.4 convert_reduce_fusion
  196.0 3.7 convolution_convert_fusion.1
  202.8 14.8 %reduce-scatter.5.cloned.1.call-done = bf16[128,768]{1,0:T(8,128)(2,1)} async-done(((bf16[512,768]{1,0:T(8,128)(2,1)}), bf16[128,768]{1,0:T(8,128)(2,1)}) %reduce-scatter.5.cloned.1.call-update) | async-done | bytes 196624 | tf_op jit(solution)/shard_map/reduce_scatter | solution.py:235
  220.0 2.0 fusion.53
  222.5 21.4 %reduce-scatter.3.cloned.1.call-done = bf16[128,768]{1,0:T(8,128)(2,1)} async-done(((bf16[512,768]{1,0:T(8,128)(2,1)}), bf16[128,768]{1,0:T(8,128)(2,1)}) %reduce-scatter.3.cloned.1.call-update) | async-done | bytes 196624 | tf_op jit(solution)/shard_map/reduce_scatter | solution.py:217
  243.9 3.0 multiply_reduce_fusion
  250.7 8.7 %all_to_all.138 = bf16[128,4,192]{0,2,1:T(8,128)(2,1)S(1)} all-to-all(bf16[128,4,192]{0,2,1:T(8,128)(2,1)} %bitcast.240), channel_id=1, replica_groups=mesh['seq'=8,'tp'=4] {'tp'}, dimensions={1} | all-to-all | bytes 393216 | tf_op jit(solution)/shard_map/all_to_all | solution.py:127
  268.3 32.4 %all_gather.29 = f32[4096,3]{0,1:T(4,128)} all-gather(f32[512,3]{0,1:T(4,128)S(1)} %bitcast.248), channel_id=1, replica_groups=mesh['seq'=8,'tp'=4] {'seq'}, dimensions={0}, use_global_device_ids=true | all-gather | bytes 55296 | tf_op jit(solution)/shard_map/all_gather | solution.py:273
  300.8 3.7 fusion.89
  304.5 2.4 fusion.78
  311.5 32.6 %all_gather.31 = f32[4096,3]{0,1:T(4,128)} all-gather(f32[512,3]{0,1:T(4,128)S(1)} %multiply_reduce_fusion.5), channel_id=1, replica_groups=mesh['seq'=8,'tp'=4] {'seq'}, dimensions={0}, use_global_device_ids=true | all-gather | bytes 55296 | tf_op jit(solution)/shard_map/all_gather | solution.py:274
  344.1 38.9 %while.49 = (s32[]{:T(128)}, f32[512,3,64]{0,2,1:T(8,128)}, bf16[4096,192]{0,1:T(8,128)(2,1)}, bf16[512,3,64]{0,2,1:T(8,128)(2,1)}, f32[3,512]{1,0:T(4,128)}, /*...) while((s32[]{:T(128)}, f32[512,3,64]{0,2,1:T(8,128)}, ...), condition=%wide.region_14.15_spmd.clone, body=%wide.region_13.14_spmd.clone.sunk | while | flops 1223983104 | bytes 35819780 | solution.py:65
  344.1 2.5 constant_dynamic-slice_fusion.10
  346.7 6.4 fusion.163
  353.1 10.5 %fusion.164 = f32[512,3,64]{0,2,1:T(8,128)} fusion(bf16[2048,3,64]{0,2,1:T(8,128)(2,1)} %bitcast.225, f32[3,2048,512]{2,1,0:T(8,128)} %fusion.163, f32[3,512]{1,0:T(4,128)S(1)} %get-tuple-element.942, f32[3,512]{1,0:T(4,128)S(1)} %copy-done.49, bf16[2048,3,64]{0,2,1:T(8,128)(2,1)} %bitcast.228, bf16[512,3,64]{0,2,1:T(8,128)(2,1)} %get-tuple-element.941, ...), kind=kOutput, calls=%fused_computation.22.clone.1 | convolution fusion | flops 821329920 | bytes 15151105 | tf_op jit(solution)/shard_map/while/body/eval_jaxpr/hqk,khd->qhd/dot_general | solution.py:99
  363.6 2.4 constant_dynamic-slice_fusion.10
  366.0 6.4 fusion.163
  372.4 10.6 %fusion.164 = f32[512,3,64]{0,2,1:T(8,128)} fusion(bf16[2048,3,64]{0,2,1:T(8,128)(2,1)} %bitcast.225, f32[3,2048,512]{2,1,0:T(8,128)} %fusion.163, f32[3,512]{1,0:T(4,128)S(1)} %get-tuple-element.942, f32[3,512]{1,0:T(4,128)S(1)} %copy-done.49, bf16[2048,3,64]{0,2,1:T(8,128)(2,1)} %bitcast.228, bf16[512,3,64]{0,2,1:T(8,128)(2,1)} %get-tuple-element.941, ...), kind=kOutput, calls=%fused_computation.22.clone.1 | convolution fusion | flops 821329920 | bytes 15151105 | tf_op jit(solution)/shard_map/while/body/eval_jaxpr/hqk,khd->qhd/dot_general | solution.py:99
  383.0 1.9 all_to_all.116
  384.8 1.8 copy.80
  386.6 13.4 %all-to-all-start.5 = ((f32[4,128,192]{1,2,0:T(8,128)}), f32[4,128,192]{1,2,0:T(8,128)}, u32[]{:S(2)}, u32[]{:S(2)}) async-start(f32[4,128,192]{1,2,0:T(8,128)} %copy.80), calls=%async_computation.7 | async-start | bytes 786432 | tf_op jit(solution)/shard_map/all_to_all | solution.py:131
  400.0 53.2 %while.50 = (s32[]{:T(128)}, f32[512,3,64]{0,2,1:T(8,128)}, f32[512,3,64]{0,2,1:T(8,128)}, bf16[4096,192]{0,1:T(8,128)(2,1)}, bf16[512,3,64]{0,2,1:T(8,128)(2,1)...) while((s32[]{:T(128)}, f32[512,3,64]{0,2,1:T(8,128)}, ...), condition=%wide.region_16.17_spmd.clone, body=%wide.region_15.16_spmd.clone.sunk | while | flops 1636270080 | bytes 50503980 | solution.py:65
  400.1 2.5 constant_dynamic-slice_fusion.11
  402.6 6.4 fusion.172
  409.6 6.9 fusion.174
  416.6 10.1 %fusion.173 = f32[512,3,64]{0,2,1:T(8,128)} fusion(bf16[2048,3,64]{0,2,1:T(8,128)(2,1)} %bitcast.223, f32[3,2048,512]{2,1,0:T(8,128)} %fusion.172, f32[3,2048]{1,0:T(4,128)} %get-tuple-element.836, f32[3,2048]{1,0:T(4,128)} %get-tuple-element.837, bf16[2048,3,64]{0,2,1:T(8,128)(2,1)} %bitcast.221, bf16[512,3,64]{0,2,1:T(8,128)(2,1)} %get-tuple-element.905, ...), kind=kOutput, calls=%fused_computation.36.clone.1 | convolution fusion | flops 821329920 | bytes 15187969 | tf_op jit(solution)/shard_map/while/body/eval_jaxpr/hqk,qhd->khd/dot_general | solution.py:120
  426.7 2.4 constant_dynamic-slice_fusion.11
  429.1 6.4 fusion.172
  436.2 7.0 fusion.174
  443.2 10.1 %fusion.173 = f32[512,3,64]{0,2,1:T(8,128)} fusion(bf16[2048,3,64]{0,2,1:T(8,128)(2,1)} %bitcast.223, f32[3,2048,512]{2,1,0:T(8,128)} %fusion.172, f32[3,2048]{1,0:T(4,128)} %get-tuple-element.836, f32[3,2048]{1,0:T(4,128)} %get-tuple-element.837, bf16[2048,3,64]{0,2,1:T(8,128)(2,1)} %bitcast.221, bf16[512,3,64]{0,2,1:T(8,128)(2,1)} %get-tuple-element.905, ...), kind=kOutput, calls=%fused_computation.36.clone.1 | convolution fusion | flops 821329920 | bytes 15187969 | tf_op jit(solution)/shard_map/while/body/eval_jaxpr/hqk,qhd->khd/dot_general | solution.py:120
  453.3 1.9 all_to_all.121
  455.2 1.8 copy.85
  457.0 4.1 all-to-all-start.6
  461.2 3.0 fusion.65
  468.6 4.0 all-to-all-start.7
  474.1 2.0 add_convert_fusion.1
  476.1 2.0 all-to-all-done.7
  478.1 5.5 fusion.62
  483.6 22.6 %psum.77 = f32[768]{0:T(1024)} all-reduce(f32[768]{0:T(1024)} %get-tuple-element.611), channel_id=1, replica_groups=mesh['seq'=8,'tp'=4] {'seq'}, use_global_device_ids=true, to_apply=%region_36.37 | all-reduce | flops 768 | bytes 6144 | tf_op jit(solution)/shard_map/psum | solution.py:344
  506.3 3.3 multiply_reduce_fusion.1
  511.0 39.8 %all-reduce.4 = (f32[768]{0:T(1024)}, f32[768]{0:T(1024)}, f32[768]{0:T(1024)}, f32[4608]{0:T(1024)}, f32[768]{0:T(1024)}) all-reduce(f32[768]{0:T(1024)S(1)} %get-tuple-element.617, f32[768]{0:T(1024)} %get-tuple-element.546, f32[768]{0:T(1024)} %get-tuple-element.549, ...), channel_id=1, replica_groups=mesh['seq'=8,'tp'=4] {'seq','tp'}, use_global_device_ids=true, to_apply=%region_20.21 | all-reduce | flops 7680 | bytes 61440 | tf_op jit(solution)/shard_map/psum | solution.py:332
  550.8 2.4 broadcast_multiply_fusion
  553.2 155.6 %all-reduce.10.cloned.1.call-done = (f32[768,2304]{1,0:T(8,128)}, f32[768,768]{1,0:T(8,128)}) async-done(((f32[768,2304]{1,0:T(8,128)}, f32[768,768]{1,0:T(8,128)}), (f32[768,2304]{1,0:T(8,128)}, f32[768,768]{1,0:T(8,128)})) %all-reduce.10.cloned.1.call-update) | async-done | bytes 9437200 | tf_op jit(solution)/shard_map/psum | solution.py:332
  708.8 6.6 copy.136
  (286 shorter events, 70.0 us)
Async XLA Ops:
  7.2 8.9 %copy-start = (bf16[768,2304]{1,0:T(8,128)(2,1)S(1)}, bf16[768,2304]{1,0:T(8,128)(2,1)}, u32[]{:S(2)}) copy-start(bf16[768,2304]{1,0:T(8,128)(2,1)} %param.32) | copy-start | bytes 10616836
  7.2 8.3 %copy-start.60 = (bf16[4608]{0:T(1024)(128)(2,1)S(1)}, bf16[4608]{0:T(1024)(128)(2,1)}, u32[]{:S(2)}) copy-start(bf16[4608]{0:T(1024)(128)(2,1)} %param.31) | copy-start | bytes 27652
  7.2 69.7 %all-gather.5.cloned.1.call-start = ((), (), s32[]{:S(2)}) async-start(), calls=%async_computation.10 | async-start | bytes 1769472 | tf_op jit(solution)/shard_map/all_gather | solution.py:182
  9.2 8.6 %copy-start.28 = (f32[768]{0:T(1024)}, f32[768]{0:T(1024)S(1)}, u32[]{:S(2)}) copy-start(f32[768]{0:T(1024)S(1)} %convert_element_type.135) | copy-start | bytes 9220
  9.2 6.9 copy-start.66
  9.2 6.9 copy-start.8
  9.9 7.9 %copy-start.45 = (f32[128]{0:T(128)}, f32[128]{0:T(128)S(1)}, u32[]{:S(2)}) copy-start(f32[128]{0:T(128)S(1)} %and_convert_fusion) | copy-start | bytes 1540
  11.0 6.7 copy-start.57
  12.2 5.6 copy-start.61
  16.1 29.3 %copy-start.47 = (f32[768]{0:T(1024)}, f32[768]{0:T(1024)S(1)}, u32[]{:S(2)}) copy-start(f32[768]{0:T(1024)S(1)} %get-tuple-element.655) | copy-start | bytes 9220
  31.2 91.9 %all-gather.7.cloned.1.call-start = ((), (), s32[]{:S(2)}) async-start(), calls=%async_computation.11 | async-start | bytes 1769472 | tf_op jit(solution)/shard_map/all_gather | solution.py:183
  41.4 15.1 %all-to-all-start.1 = ((bf16[128,4,192]{0,2,1:T(8,128)(2,1)}), bf16[128,4,192]{0,2,1:T(8,128)(2,1)}, u32[]{:S(2)}, u32[]{:S(2)}) async-start(bf16[128,4,192]{0,2,1:T(8,128)(2,1)} %get-tuple-element.643), calls=%async_computation.1 | async-start | bytes 393216 | tf_op jit(solution)/shard_map/all_to_all | solution.py:127
  131.9 8.5 %copy-start.1 = (f32[3,2048,512]{2,1,0:T(8,128)S(1)}, f32[3,2048,512]{2,1,0:T(8,128)}, u32[]{:S(2)}) copy-start(f32[3,2048,512]{2,1,0:T(8,128)} %get-tuple-element.813) | copy-start | bytes 37748740 | tf_op jit(solution)/shard_map/while
  152.0 8.6 %copy-start.1 = (f32[3,2048,512]{2,1,0:T(8,128)S(1)}, f32[3,2048,512]{2,1,0:T(8,128)}, u32[]{:S(2)}) copy-start(f32[3,2048,512]{2,1,0:T(8,128)} %get-tuple-element.813) | copy-start | bytes 37748740 | tf_op jit(solution)/shard_map/while
  168.3 9.4 %all-to-all-start.3 = ((bf16[4,128,192]{1,2,0:T(8,128)(2,1)}), bf16[4,128,192]{1,2,0:T(8,128)(2,1)}, u32[]{:S(2)}, u32[]{:S(2)}) async-start(bf16[4,128,192]{1,2,0:T(8,128)(2,1)} %copy.77), calls=%async_computation.3 | async-start | bytes 393216 | tf_op jit(solution)/shard_map/all_to_all | solution.py:131
  172.3 5.4 copy-start.29
  172.3 45.2 %reduce-scatter.5.cloned.1.call-start = ((), (), s32[]{:S(2)}) async-start(), calls=%async_computation.13 | async-start | bytes 983040 | tf_op jit(solution)/shard_map/reduce_scatter | solution.py:235
  172.7 3.5 copy-start.67
  172.7 4.1 copy-start.68
  176.2 5.0 copy-start.40
  177.7 12.2 %copy-start.75 = (f32[512,768]{1,0:T(8,128)S(1)}, f32[512,768]{1,0:T(8,128)}, u32[]{:S(2)}) copy-start(f32[512,768]{1,0:T(8,128)} %fusion.88) | copy-start | bytes 4718596
  180.3 9.6 %copy-start.64 = (f32[768]{0:T(1024)S(1)}, f32[768]{0:T(1024)}, u32[]{:S(2)}) copy-start(f32[768]{0:T(1024)} %convert_element_type.149) | copy-start | bytes 9220
  180.3 9.6 %copy-start.74 = (bf16[768,768]{1,0:T(8,128)(2,1)S(1)}, bf16[768,768]{1,0:T(8,128)(2,1)}, u32[]{:S(2)}) copy-start(bf16[768,768]{1,0:T(8,128)(2,1)} %param.34) | copy-start | bytes 3538948
  180.4 13.0 %copy-start.59 = (f32[128]{0:T(128)}, f32[128]{0:T(128)S(1)}, u32[]{:S(2)}) copy-start(f32[128]{0:T(128)S(1)} %broadcast_multiply_fusion.4) | copy-start | bytes 1540
  195.9 48.0 %reduce-scatter.3.cloned.1.call-start = ((), (), s32[]{:S(2)}) async-start(), calls=%async_computation.12 | async-start | bytes 983040 | tf_op jit(solution)/shard_map/reduce_scatter | solution.py:217
  196.0 21.5 %copy-start.42 = (f32[768]{0:T(1024)S(1)}, f32[768]{0:T(1024)}, u32[]{:S(2)}) copy-start(f32[768]{0:T(1024)} %convert_element_type.147) | copy-start | bytes 9220
  199.7 200.3 %all-gather.9.cloned.1.call-start = ((), (), s32[]{:S(2)}) async-start(), calls=%async_computation.14 | async-start | bytes 1769472 | tf_op jit(solution)/shard_map/all_gather | solution.py:298
  201.4 198.6 %all-gather.11.cloned.1.call-start = ((), (), s32[]{:S(2)}) async-start(), calls=%async_computation.15 | async-start | bytes 1769472 | tf_op jit(solution)/shard_map/all_gather | solution.py:299
  243.9 3.8 copy-start.13
  243.9 3.8 copy-start.43
  248.9 18.8 %copy-start.27 = (f32[3,512]{1,0:T(4,128)S(1)}, f32[3,512]{1,0:T(4,128)}, u32[]{:S(2)}) copy-start(f32[3,512]{1,0:T(4,128)} %get-tuple-element.434) | copy-start | bytes 18436
  260.8 292.4 %all-reduce.12.cloned.1.call-start = ((), (), s32[]{:S(2)}) async-start(), calls=%async_computation.17 | async-start | bytes 9437184 | tf_op jit(solution)/shard_map/psum | solution.py:344
  300.8 3.7 copy-start.23
  300.8 3.7 copy-start.76
  346.7 6.4 copy-start.3
  346.7 6.4 copy-start.49
  366.0 6.4 copy-start.3
  366.0 6.4 copy-start.49
  386.6 70.4 %all-to-all-start.5 = ((f32[4,128,192]{1,2,0:T(8,128)}), f32[4,128,192]{1,2,0:T(8,128)}, u32[]{:S(2)}, u32[]{:S(2)}) async-start(f32[4,128,192]{1,2,0:T(8,128)} %copy.80), calls=%async_computation.7 | async-start | bytes 786432 | tf_op jit(solution)/shard_map/all_to_all | solution.py:131
  402.6 6.4 copy-start.2
  402.6 6.4 copy-start.21
  402.6 6.4 copy-start.22
  429.1 6.4 copy-start.2
  429.1 6.4 copy-start.21
  429.1 6.4 copy-start.22
  453.3 7.9 %copy-start.44 = (f32[768]{0:T(1024)S(1)}, f32[768]{0:T(1024)}, u32[]{:S(2)}) copy-start(f32[768]{0:T(1024)} %get-tuple-element.660) | copy-start | bytes 9220
  457.0 11.6 %all-to-all-start.6 = ((f32[4,128,192]{1,2,0:T(8,128)}), f32[4,128,192]{1,2,0:T(8,128)}, u32[]{:S(2)}, u32[]{:S(2)}) async-start(f32[4,128,192]{1,2,0:T(8,128)} %copy.85), calls=%async_computation.8 | async-start | bytes 786432 | tf_op jit(solution)/shard_map/all_to_all | solution.py:131
  468.6 9.4 %all-to-all-start.7 = ((bf16[4,128,192]{1,2,0:T(8,128)(2,1)}), bf16[4,128,192]{1,2,0:T(8,128)(2,1)}, u32[]{:S(2)}, u32[]{:S(2)}) async-start(bf16[4,128,192]{1,2,0:T(8,128)(2,1)} %copy.86), calls=%async_computation.9 | async-start | bytes 393216 | tf_op jit(solution)/shard_map/all_to_all | solution.py:131
  472.7 236.1 %all-reduce.10.cloned.1.call-start = ((), (), s32[]{:S(2)}) async-start(), calls=%async_computation.16 | async-start | bytes 18874368 | tf_op jit(solution)/shard_map/psum | solution.py:332
  474.0 4.1 copy-start.30
  474.0 4.1 copy-start.35
  474.0 4.1 copy-start.37
  474.0 4.0 copy-start.39
  483.6 22.6 %copy-start.46 = (f32[128]{0:T(128)S(1)}, f32[128]{0:T(128)}, u32[]{:S(2)}) copy-start(f32[128]{0:T(128)} %copy-done.45) | copy-start | bytes 1540
  506.2 3.4 copy-start.56
  506.2 3.5 copy-start.54
  506.2 3.5 copy-start.53
  506.2 3.5 copy-start.55
  506.2 3.5 copy-start.71
  506.2 3.5 copy-start.9
  506.3 3.5 copy-start.58
  506.3 3.5 copy-start.62
  506.3 3.8 copy-start.11
  708.8 6.6 copy-start.17
  (37 other events, 57.9 us)
Sparse Core Ops, SparseCore 0:
  31.3 45.5 all-gather.4
  79.6 43.4 all-gather.6
  196.1 21.4 reduce-scatter.4
  220.7 23.2 reduce-scatter.2
  245.8 46.6 all-gather.8
  294.4 43.1 all-gather.10
  341.8 168.4 all-reduce.11
  517.4 191.3 all-reduce.9

commit v2 on v1

--- a/solution.py
+++ b/solution.py
@@ -1,8 +1,12 @@
+import functools
 import math
 
 import jax
 import jax.numpy as jnp
+import numpy as np
 from jax import lax
+from jax.experimental import pallas as pl
+from jax.experimental.pallas import tpu as pltpu
 from jax.sharding import PartitionSpec as P
 
 HEADS = 12
@@ -359,7 +363,1058 @@
     )
 
 
+VMEM_LIMIT = 63 * 2**20
+GROUPS = 4
+CHIPS = 4
+MESH = pl.DeviceIdType.MESH
+f32, bf16 = jnp.float32, jnp.bfloat16
+
+
+def dot(left, right, left_dim, right_dim):
+    return lax.dot_general(
+        left, right, (((left_dim,), (right_dim,)), ((), ())), preferred_element_type=f32
+    )
+
+
+def normalise(rows):
+    centred = rows - jnp.mean(rows, axis=-1, keepdims=True)
+    variance = jnp.mean(centred * centred, axis=-1, keepdims=True)
+    spread = lax.rsqrt(variance + epsilon)
+    return centred * spread, spread
+
+
+def normalise_back(upstream, normal, spread):
+    along = jnp.mean(upstream * normal, axis=-1, keepdims=True)
+    return spread * (upstream - jnp.mean(upstream, axis=-1, keepdims=True) - normal * along)
+
+
+def column_sum(rows):
+    return jnp.sum(rows, axis=0, keepdims=True)
+
+
+def row_of(ref, i, width):
+    return ref[i * width : (i + 1) * width].astype(f32).reshape(1, width)
+
+
+def activation_of(step, first, count, cond):
+    halfway = cond // 2
+    place = first + lax.broadcasted_iota(jnp.int32, (count, 1), 0)
+    which = jnp.where(place < halfway, place, place - halfway).astype(f32)
+    angles = step.astype(f32) * jnp.exp(-math.log(10000.0) * which / halfway)
+    wave = jnp.where(place < halfway, jnp.cos(angles), jnp.sin(angles))
+    return wave / (1.0 + jnp.exp(-wave))
+
+
+def finish_kernel(
+    per,
+    head,
+    timestep_ref,
+    sums,
+    output,
+    input_grad,
+    first,
+    second,
+    out_parts,
+    up_parts,
+    down_parts,
+    o_out,
+    o_in,
+    o_embed,
+    o_gain1,
+    o_gain2,
+    o_ada,
+    o_ada_b,
+    o_qkv,
+    o_ow,
+    o_up,
+    o_up_b,
+    o_down,
+    o_down_b,
+):
+    n = pl.program_id(0)
+    width = sums.shape[1]
+    o_out[...] = output[...]
+    o_in[...] = input_grad[...]
+    o_up[...] = up_parts[...].astype(f32)
+    o_down[...] = down_parts[...].astype(f32)
+    wide = out_parts.shape[3]
+    for m in range(2):
+        o_ow[:, m * wide : (m + 1) * wide] = out_parts[0, m].astype(f32)
+    count = o_ada.shape[0]
+    act = activation_of(timestep_ref[0], n * count, count, count * 8)
+    for i in range(6):
+        o_ada[:, i * width : (i + 1) * width] = act * sums[8 + i : 9 + i, :]
+
+    def piece(third, j):
+        g, h = j // per, j % per
+        source = first if h < 2 else second
+        a = (4 + h % 2) * head if third == 0 else h % 2 * 2 * head + (third - 1) * head
+        if h == 2 and third == 0:
+            a = 2 * head
+        return source[g, 0, :, a : a + head].astype(f32)
+
+    for third in range(3):
+        for j in range(0, GROUPS * per, 2):
+            a = third * width + j * head
+            o_qkv[:, a : a + 2 * head] = jnp.concatenate(
+                [piece(third, j), piece(third, j + 1)], axis=1
+            )
+
+    @pl.when(n == 0)
+    def _():
+        for ref, i in ((o_embed, 0), (o_gain1, 1), (o_gain2, 2), (o_down_b, 3), (o_up_b, 4)):
+            ref[...] = sums[i : i + 1, :].reshape(width)
+        for i in range(6):
+            o_ada_b[i * width : (i + 1) * width] = sums[8 + i : 9 + i, :].reshape(width)
+
+
+def fused_kernel(
+    tp_size,
+    prefix_ref,
+    timestep_ref,
+    flags_ref,
+    embed_ref,
+    gain1_ref,
+    gain2_ref,
+    up_b_ref,
+    down_b_ref,
+    ada_b_ref,
+    tokens_ref,
+    cot_ref,
+    cos_hbm,
+    sin_hbm,
+    ada_hbm,
+    qkv_hbm,
+    out_w,
+    up_w,
+    down_w,
+    o_out,
+    o_in,
+    o_vec,
+    o_qkv1,
+    o_qkv2,
+    o_ow,
+    o_mlp,
+    mod,
+    start,
+    normal1,
+    spread1,
+    normal2,
+    spread2,
+    branch,
+    middle_grad,
+    mcol,
+    nl,
+    nt,
+    whm,
+    cosb,
+    sinb,
+    kvall,
+    qd,
+    expd,
+    tops,
+    mrun,
+    lrun,
+    ot,
+    lse,
+    delta,
+    mtb,
+    mi,
+    rg,
+    ng,
+    acts,
+    hgs,
+    ag,
+    pn_own,
+    pn_so,
+    pn_si,
+    pn_yo,
+    pn_yi,
+    bgg,
+    mig,
+    dob,
+    doi,
+    dos,
+    sbo,
+    sbi,
+    rso,
+    rsi,
+    dkv,
+    pg1,
+    pgi1,
+    pg2,
+    pgi2,
+    dwb1,
+    dws1,
+    dwc1,
+    dwr1,
+    wg1,
+    dwb2,
+    dws2,
+    dwc2,
+    dwr2,
+    wg2,
+    wbuf,
+    wsi,
+    wz,
+    wgt,
+    og,
+    mbuf,
+    msi,
+    mz,
+    mgat,
+    vec,
+    vpl,
+    vzs,
+    vco,
+    ss,
+    rr,
+    ls,
+):
+    rows, width = tokens_ref.shape
+    head = width // HEADS
+    per = HEADS // GROUPS
+    gw = per * head
+    line = GROUPS * rows
+    shard = width // (2 * CHIPS)
+    kv_at = [0, 2 * head, 6 * head]
+    q_at = [4 * head, 8 * head]
+    split = 6 * head
+    s, t = lax.axis_index("seq"), lax.axis_index("tp")
+    z, x, y, c = s // 2, s % 2, t // 2, t % 2
+    sib = (s, t + 1 - 2 * c)
+    chip = x * 2 + y
+    p = chip * 2 + c
+
+    def chip_of(k):
+        return ((x + k // 2) % 2) * 2 + (y + k % 2) % 2
+
+    def dev(k):
+        return (z * 2 + (x + k // 2) % 2, ((y + k % 2) % 2) * 2 + c)
+
+    def zdev(k):
+        return (((z + k) % 4) * 2 + x, t)
+
+    def zfrom(k):
+        return (z + 4 - k) % 4
+
+    names = {}
+
+    def ids(name, count):
+        if name not in names:
+            names[name] = sum(n for _, n in names.values()), count
+        return names[name][0]
+
+    def remote(src, dst, i, to):
+        return pltpu.make_async_remote_copy(
+            src_ref=src,
+            dst_ref=dst,
+            send_sem=ss.at[i],
+            recv_sem=rr.at[i],
+            device_id=to,
+            device_id_type=MESH,
+        )
+
+    pending = []
+
+    def send(src, dst, i, to):
+        copy = remote(src, dst, i, to)
+        copy.start()
+        pending.append(copy)
+        return copy
+
+    barrier = pltpu.get_barrier_semaphore()
+    t_sib, t_y = y * 2 + 1 - c, (1 - y) * 2 + c
+    t_ysib = (1 - y) * 2 + 1 - c
+    ysib = (s, t_ysib)
+    peers = [sib, ysib] + [dev(k) for k in (1, 2, 3)] + [zdev(k) for k in (1, 2, 3)]
+    for peer in peers:
+        pl.semaphore_signal(barrier, inc=1, device_id=peer, device_id_type=MESH)
+
+    locals_ = []
+
+    def local(src, dst, i):
+        copy = pltpu.make_async_copy(src, dst, ls.at[i])
+        copy.start()
+        locals_.append(copy)
+        return copy
+
+    cond = ada_hbm.shape[0]
+    ada = [
+        local(ada_hbm.at[:, i * width : (i + 1) * width], msi.at[i * cond : (i + 1) * cond], 11 + i)
+        for i in range(6)
+    ]
+    stage = [mbuf.at[0:width], mbuf.at[width : 2 * width], mgat.at[0:width]]
+    raw = [local(qkv_hbm.at[:, i * width : (i + 1) * width], stage[i], i) for i in range(3)]
+    for zb in range(GROUPS):
+        block = (zb * 2 + x) * tp_size + t
+        raw.append(local(cos_hbm.at[block], cosb.at[zb], 3 + zb))
+        raw.append(local(sin_hbm.at[block], sinb.at[zb], 7 + zb))
+
+    act = activation_of(timestep_ref[0], 0, cond, cond)
+    for i in range(6):
+        ada[i].wait()
+        part = msi[i * cond : (i + 1) * cond, :].astype(f32)
+        mod[i : i + 1, :] = column_sum(part * act) + row_of(ada_b_ref, i, width)
+    shift1, scale1, gate1 = mod[0:1, :], mod[1:2, :], mod[2:3, :]
+    shift2, scale2, gate2 = mod[3:4, :], mod[4:5, :], mod[5:6, :]
+    embed, gain1, gain2, up_b, down_b = (
+        row_of(ref, 0, width) for ref in (embed_ref, gain1_ref, gain2_ref, up_b_ref, down_b_ref)
+    )
+    place = (s * tp_size + t) * rows + lax.broadcasted_iota(jnp.int32, (1, rows), 1)
+    chosen = jnp.where((place >= prefix_ref[0]) & (flags_ref[...].reshape(1, rows) == 1), 1.0, 0.0).astype(f32)
+    mcol[...] = jnp.broadcast_to(chosen, (rows, rows)).T[:, 0:1]
+    start[...] = tokens_ref[...].astype(f32) + mcol[...] * embed
+    normal, spread = normalise(start[...])
+    normal1[...] = normal
+    spread1[...] = spread
+    nl[z] = (normal * (gain1 * (1.0 + scale1)) + shift1).astype(bf16)
+    rg[t] = (cot_ref[...].astype(f32) * gate2).astype(bf16)
+
+    pl.semaphore_wait(barrier, len(peers))
+    zi = ids("nl", 3)
+    got_nl = [send(nl.at[z], nl.at[z], zi + k - 1, zdev(k)) for k in (1, 2, 3)]
+
+    def group_start(buffer, name):
+        i = ids(name, 3)
+        one = send(buffer.at[t], buffer.at[t], i, sib)
+        two = send(buffer.at[t], buffer.at[t], i + 1, dev(1))
+        return one, two, i + 2
+
+    def group_pass(buffer, two, i):
+        two.wait_recv()
+        other = (1 - y) * 2 + c
+        return send(buffer.at[other], buffer.at[other], i, sib)
+
+    rg1, rg2, rgi = group_start(rg, "rg")
+
+    for copy in raw:
+        copy.wait()
+    for g in range(GROUPS):
+        for h in range(per):
+            a = g * gw + h * head
+            tile = [mbuf[width : 2 * width, a : a + head], mgat[0:width, a : a + head]]
+            whm[g, :, kv_at[h] : kv_at[h] + 2 * head] = jnp.concatenate(tile, axis=1)
+        a = g * gw
+        whm[g, :, q_at[0] : q_at[0] + 2 * head] = mbuf[0:width, a : a + 2 * head]
+        tile = [mbuf[0:width, a + 2 * head : a + 3 * head], jnp.zeros((width, head), bf16)]
+        whm[g, :, q_at[1] : q_at[1] + 2 * head] = jnp.concatenate(tile, axis=1)
+
+    lane = lax.broadcasted_iota(jnp.int32, (rows, 2 * head), 1)
+    low_half = lane < head
+    first = (lane % head) < head // 2
+    half = head // 2
+
+    def turn(tile, cosine, sine):
+        ahead = jnp.where(first, -pltpu.roll(tile, 2 * head - half, 1), pltpu.roll(tile, half, 1))
+        return tile * cosine + ahead * sine
+
+    def turn_back(tile, cosine, sine):
+        moved = tile * sine
+        behind = jnp.where(first, pltpu.roll(moved, 2 * head - half, 1), -pltpu.roll(moved, half, 1))
+        return tile * cosine + behind
+
+    kvi = ids("kv", 12)
+    scale = head ** (-0.5)
+    for k in range(GROUPS):
+        zb = zfrom(k)
+        if k:
+            got_nl[k - 1].wait_recv()
+        proj = dot(nl[zb], whm[z], 1, 0)
+        cosine, sine = cosb[zb], sinb[zb]
+        here = pl.ds(zb * rows, rows)
+        for h in range(per):
+            tile = proj[:, kv_at[h] : kv_at[h] + 2 * head]
+            kvall[h, p, here, :] = jnp.where(low_half, turn(tile, cosine, sine), tile).astype(bf16)
+        for kk in (1, 2, 3):
+            src = kvall.at[:, p, here, :]
+            send(src, src, kvi + (kk - 1) * 4 + k, dev(kk))
+        for i in range(2):
+            tile = turn(proj[:, q_at[i] : q_at[i] + 2 * head], cosine, sine) * scale
+            qd[2 * i, here, :] = jnp.where(low_half, tile, 0.0).astype(bf16)
+            if i == 0:
+                qd[1, here, :] = jnp.where(low_half, pltpu.roll(tile, head, 1), 0.0).astype(bf16)
+    kdi = ids("kvd", 4)
+    remote(kvall.at[:, p], kvall.at[:, p], kdi, sib).start()
+
+    mrun[...] = jnp.full_like(mrun, floor_value)
+    lrun[...] = jnp.zeros_like(lrun)
+    ot[...] = jnp.zeros_like(ot)
+
+    def forward(i, carry):
+        k, r = i // (2 * per), i % (2 * per)
+        h, away = r % per, r // per
+        chunk = chip_of(k) * 2 + (c + away) % 2
+
+        @pl.when((r == 0) & (k > 0))
+        def _():
+            for q in range(GROUPS):
+                block = kvall.at[:, chunk, pl.ds(q * rows, rows), :]
+                remote(block, block, kvi + (k - 1) * 4 + q, sib).wait_recv()
+            remote(kvall.at[:, chunk], kvall.at[:, chunk], kdi + k, sib).start()
+
+        @pl.when(r == per)
+        def _():
+            remote(kvall.at[:, chunk], kvall.at[:, chunk], kdi + k, sib).wait_recv()
+
+        keys = kvall[h, chunk]
+        scores = dot(keys, qd[h], 1, 1)
+        before = mrun[h]
+        top = jnp.maximum(before, jnp.max(scores, axis=0, keepdims=True))
+        weights = jnp.exp(scores - top)
+        factor = jnp.exp(before - top)
+        rounded = weights.astype(bf16)
+        expd[h, chunk] = rounded
+        lrun[h] = lrun[h] * factor + column_sum(weights)
+        mrun[h] = top
+        tops[h, chunk] = top
+        ot[h] = ot[h] * factor + dot(keys, rounded, 0, 0)
+        return carry
+
+    lax.fori_loop(0, 2 * CHIPS * per, forward, 0)
+
+    for h in range(per):
+        ot[h] = ot[h] / lrun[h]
+        lse[h] = mrun[h] + jnp.log(lrun[h])
+        for zb in range(GROUPS):
+            mtb[zb, h * head : (h + 1) * head, :] = ot[
+                h, head : 2 * head, zb * rows : (zb + 1) * rows
+            ].astype(bf16)
+    i = ids("mix", 3)
+    got_mix = [send(mtb.at[(z + k) % 4], mi.at[z], i + k - 1, zdev(k)) for k in (1, 2, 3)]
+    mi[z] = mtb[z]
+    rg3 = group_pass(rg, rg2, rgi)
+    nt[...] = nl[...].reshape(line, width).T
+    rg1.wait_recv()
+    rg3.wait_recv()
+    for tb in range(tp_size):
+        ag[tb] = dot(rg[tb], down_w[...], 1, 1)
+    for copy in got_mix:
+        copy.wait_recv()
+    total = dot(mi[0], out_w[0:gw, :], 0, 0)
+    for g in range(1, GROUPS):
+        total = total + dot(mi[g], out_w[g * gw : (g + 1) * gw, :], 0, 0)
+    i = ids("mig", 3)
+    to = ((t_sib, sib), (t_y, dev(1)), (t_ysib, ysib))
+    got_mig = [send(mi.at[at], mig.at[t], i + n, where) for n, (at, where) in enumerate(to)]
+    mig[t] = mi[t]
+    branch[...] = total
+    start[...] = start[...] + gate1 * total
+    normal, spread = normalise(start[...])
+    normal2[...] = normal
+    spread2[...] = spread
+    ng[t] = (normal * (gain2 * (1.0 + scale2)) + shift2).astype(bf16)
+    ng1, ng2, ngi = group_start(ng, "ng")
+
+    inner, cubic = 0.7978845608028654, 0.044715
+
+    def feed(tb):
+        hidden = dot(ng[tb], up_w[...], 1, 0) + up_b
+        square = hidden * hidden
+        bent = jnp.tanh(inner * hidden * (1.0 + cubic * square))
+        share = 0.5 * (1.0 + bent)
+        acts[tb] = (hidden * share).astype(bf16)
+        slope = share + 0.5 * hidden * (1.0 - bent * bent) * (
+            inner * (1.0 + 3.0 * cubic * square)
+        )
+        hgs[tb] = (ag[tb] * slope).astype(bf16)
+        return dot(hgs[tb], up_w[...], 1, 1)
+
+    def group_sum(n, term, name, own_first, sib_first, y_first, ysib_first):
+        i = ids(name, 3)
+        if own_first is not None:
+            own_first()
+        pn_own[n] = term(t)
+        if sib_first is not None:
+            sib_first()
+        pn_so[n, 0] = term(t_sib).astype(bf16)
+        one = send(pn_so.at[n, 0], pn_si.at[n, 0], i, sib)
+        if ysib_first is not None:
+            y_first()
+            ysib_first()
+        pn_so[n, 1] = term(t_ysib).astype(bf16)
+        two = send(pn_so.at[n, 1], pn_si.at[n, 1], i + 1, sib)
+        mine = term(t_y)
+        two.wait_recv()
+        pn_yo[n] = (mine + pn_si[n, 1].astype(f32)).astype(bf16)
+        three = send(pn_yo.at[n], pn_yi.at[n], i + 2, dev(1))
+
+        def finish():
+            one.wait_recv()
+            three.wait_recv()
+            return pn_own[n] + pn_si[n, 0].astype(f32) + pn_yi[n].astype(f32)
+
+        return finish
+
+    ng3 = []
+    finish_grad = group_sum(
+        0,
+        feed,
+        "pn",
+        None,
+        ng1.wait_recv,
+        lambda: ng3.append(group_pass(ng, ng2, ngi)),
+        lambda: ng3[0].wait_recv(),
+    )
+    half_rows = width // 2
+
+    def exchange(part, buffer, incoming, parts, gathered, base, count, name):
+        near, own = count // 2, count // 2 // GROUPS
+        i = ids(name, 8)
+        src = buffer.at[pl.ds(base + (1 - x) * near, near)]
+        got = send(src, incoming, i, dev(2))
+        yield
+        got.wait_recv()
+        mine = buffer[pl.ds(base + x * near, near), :].astype(f32) + incoming[...].astype(f32)
+        incoming[...] = mine.astype(bf16)
+        got = []
+        for k in (1, 2, 3):
+            src = incoming.at[pl.ds(((z + k) % 4) * own, own)]
+            got.append(send(src, parts.at[k - 1], i + k, zdev(k)))
+        yield
+        for copy in got:
+            copy.wait_recv()
+        mine = incoming[pl.ds(z * own, own), :].astype(f32)
+        for k in range(3):
+            mine = mine + parts[k].astype(f32)
+        src = gathered.at[pl.ds(base + x * near + z * own, own)]
+        src[...] = mine.astype(bf16)
+        got = [send(src, src, i + 3 + k, zdev(k)) for k in (1, 2, 3)]
+        yield
+        for copy in got:
+            copy.wait_recv()
+        src = gathered.at[pl.ds(base + x * near, near)]
+        got = send(src, src, i + 7, dev(2))
+        yield
+        got.wait_recv()
+        yield
+
+    def exchange_of(m):
+        side = pl.ds(m * half_rows, half_rows)
+        return exchange(m, mbuf, msi.at[side], mz.at[m], mgat, m * width, width, f"m{m}")
+
+    def matrix(left, right):
+        return dot(left[...].reshape(line, width), right[...].reshape(line, width), 0, 0)
+
+    mbuf[width : 2 * width, :] = matrix(acts, rg).astype(bf16)
+    down_path = exchange_of(1)
+    next(down_path)
+
+    upstream = cot_ref[...].astype(f32)
+    n2g = finish_grad()
+    normal = normal2[...]
+    middle = normalise_back(n2g * (gain2 * (1.0 + scale2)), normal, spread2[...]) + upstream
+    bgg[t] = (middle * gate1).astype(bf16)
+    for g in range(GROUPS):
+        dob[g] = dot(out_w[g * gw : (g + 1) * gw, :], bgg[t], 1, 1).astype(bf16)
+    i = ids("do", 3)
+    got_do = [send(dob.at[(z + k) % 4], doi.at[z], i + k - 1, zdev(k)) for k in (1, 2, 3)]
+    bg1, bg2, bgi = group_start(bgg, "bg")
+    doi[z] = dob[z]
+    middle_grad[...] = middle
+    vec[3:4, :] = column_sum(middle * branch[...])
+    vec[4:5, :] = column_sum(n2g)
+    vec[5:6, :] = column_sum(n2g * normal)
+    mbuf[0:width, :] = matrix(ng, hgs).astype(bf16)
+    up_path = exchange_of(0)
+    next(up_path)
+    finish_result = group_sum(
+        1, lambda tb: dot(acts[tb], down_w[...], 1, 0), "res", None, None, None, None
+    )
+    bg3 = group_pass(bgg, bg2, bgi)
+    vec[8:9, :] = column_sum(hgs[...].reshape(line, width).astype(f32))
+    vec[9:16, :] = jnp.zeros((7, width), f32)
+    vec[7:8, :] = column_sum(rg[t].astype(f32))
+
+    for copy in got_do:
+        copy.wait_recv()
+    for h in range(per):
+        dos[h, 0:head, :] = jnp.zeros((head, line), bf16)
+        for zb in range(GROUPS):
+            dos[h, head : 2 * head, zb * rows : (zb + 1) * rows] = doi[
+                zb, h * head : (h + 1) * head, :
+            ]
+        delta[h] = column_sum(dos[h, head : 2 * head, :].astype(f32) * ot[h, head : 2 * head, :])
+    dq = ot
+    dq[...] = jnp.zeros_like(dq)
+    sbx = ids("sb", 12)
+    rsx = ids("rs", 9)
+
+    def backward(i, carry):
+        h, r = i // (2 * CHIPS), i % (2 * CHIPS)
+        away, k = 1 - r // CHIPS, CHIPS - 1 - r % CHIPS
+        chunk = chip_of(k) * 2 + (c + away) % 2
+        keys = kvall[h, chunk]
+        factor = jnp.exp(tops[h, chunk] - lse[h])
+        scaled = (dos[h].astype(f32) * factor).astype(bf16)
+        prob_grad = dot(keys, scaled, 1, 0)
+        rounded = expd[h, chunk]
+        score_grad = (rounded.astype(f32) * (prob_grad - delta[h] * factor)).astype(bf16)
+        dq[h] = dq[h] + dot(keys, score_grad, 0, 0)
+        part = dot(score_grad, qd[h], 1, 0) + dot(rounded, scaled, 1, 1)
+        over = remote(sbo.at[k], sbi.at[h, k], sbx + h * CHIPS + k, sib)
+
+        @pl.when((away == 1) & (h > 0))
+        def _():
+            remote(sbo.at[k], sbi.at[h, k], sbx + (h - 1) * CHIPS + k, sib).wait_send()
+
+        @pl.when(away == 1)
+        def _():
+            sbo[k] = part.astype(bf16)
+            over.start()
+
+        @pl.when(away == 0)
+        def _():
+            over.wait_recv()
+            both = part + sbi[h, k].astype(f32)
+
+            @pl.when(k == 0)
+            def _():
+                dkv[h] = both
+
+            @pl.when((k > 0) & (h > 0))
+            def _():
+                remote(rso.at[k - 1], rsi.at[h, k - 1], rsx + (h - 1) * 3 + k - 1, sib).wait_send()
+
+            @pl.when(k > 0)
+            def _():
+                rso[k - 1] = both.astype(bf16)
+                remote(rso.at[k - 1], rsi.at[h, k - 1], rsx + h * 3 + k - 1, dev(k)).start()
+
+        return carry
+
+    def backward_from(first, last):
+        lax.fori_loop(first, last, backward, 0)
+
+    def keys_back(h, out, b):
+        total = dkv[h]
+        for k in range(3):
+            remote(rso.at[k], rsi.at[h, k], rsx + h * 3 + k, sib).wait_recv()
+            total = total + rsi[h, k].astype(f32)
+        for zb in range(GROUPS):
+            tile = total[zb * rows : (zb + 1) * rows, :]
+            back = jnp.where(low_half, turn_back(tile, cosb[zb], sinb[zb]), tile)
+            out[zb, :, b : b + 2 * head] = back.astype(bf16)
+
+    def queries_back(one, two, out, b):
+        flat = jnp.concatenate([one, two], axis=0).T * scale
+        for zb in range(GROUPS):
+            tile = flat[zb * rows : (zb + 1) * rows, :]
+            out[zb, :, b : b + 2 * head] = turn_back(tile, cosb[zb], sinb[zb]).astype(bf16)
+
+    def scatter_rows(out, into, name):
+        i = ids(name, 3)
+        got = [send(out.at[(z + k) % 4], into.at[z], i + k - 1, zdev(k)) for k in (1, 2, 3)]
+        into[z] = out[z]
+        return got
+
+    def projection(out, mine, other, summed, incoming, gathered, name):
+        grad = dot(nt[...], out[...].reshape(line, out.shape[2]), 1, 0)
+        for n in range(2 * CHIPS):
+            mine[n % 2, n // 2] = grad[n * shard : (n + 1) * shard, :].astype(bf16)
+        i = ids(name, 13)
+        got = send(mine.at[1 - c], other, i, sib)
+        yield
+        got.wait_recv()
+        summed[...] = (mine[c].astype(f32) + other[...].astype(f32)).astype(bf16)
+        got = [send(summed.at[chip_of(k)], incoming.at[k - 1], i + k, dev(k)) for k in (1, 2, 3)]
+        yield
+        for copy in got:
+            copy.wait_recv()
+        whole = summed[chip].astype(f32)
+        for k in range(3):
+            whole = whole + incoming[k].astype(f32)
+        gathered[z, chip, c] = whole.astype(bf16)
+        src = gathered.at[z, chip, c]
+        got = [send(src, src, i + 3 + k, zdev(k)) for k in (1, 2, 3)]
+        yield
+        for copy in got:
+            copy.wait_recv()
+        src = gathered.at[:, chip, c]
+        over_y = send(src, src, i + 7, dev(1))
+        over_x = send(src, src, i + 8, dev(2))
+        last = [send(src, src, i + 9, sib)]
+        yield
+        over_x.wait_recv()
+        src = gathered.at[:, chip_of(2), c]
+        both = send(src, src, i + 10, dev(1))
+        last.append(send(src, src, i + 11, sib))
+        yield
+        over_y.wait_recv()
+        src = gathered.at[:, chip_of(1), c]
+        last.append(send(src, src, i + 12, sib))
+        both.wait_recv()
+        src = gathered.at[:, chip_of(3), c]
+        last.append(send(src, src, ids(name + "x", 1), sib))
+        yield
+        for copy in last:
+            copy.wait_recv()
+        yield
+
+    next(down_path)
+    backward_from(0, 8)
+    bg1.wait_recv()
+    bg3.wait_recv()
+    for copy in got_mig:
+        copy.wait_recv()
+    grad = dot(mig[0], bgg[0], 1, 0)
+    for n in range(1, tp_size):
+        grad = grad + dot(mig[n], bgg[n], 1, 0)
+    wide = width // 2
+    wbuf[0:gw, :] = grad[:, 0:wide].astype(bf16)
+    wbuf[gw : 2 * gw, :] = grad[:, wide:width].astype(bf16)
+    out_path = exchange(2, wbuf, wsi, wz, wgt, 0, 2 * gw, "wo")
+    next(out_path)
+    result = finish_result() + down_b
+    o_out[...] = (start[...] + gate2 * result).astype(bf16)
+    vec[6:7, :] = column_sum(cot_ref[...].astype(f32) * result)
+    backward_from(8, 16)
+    next(up_path)
+    backward_from(16, 20)
+    keys_back(0, pg1, kv_at[0])
+    keys_back(1, pg1, kv_at[1])
+    queries_back(dq[0, 0:head, :], dq[1, 0:head, :], pg1, q_at[0])
+    got_pg1 = scatter_rows(pg1, pgi1, "pg1")
+    first_path = projection(pg1, dwb1, dws1, dwc1, dwr1, wg1, "w1")
+    next(first_path)
+    next(down_path)
+    backward_from(20, 24)
+    next(first_path)
+    next(out_path)
+    keys_back(2, pg2, kv_at[2] - split)
+    queries_back(dq[2, 0:head, :], jnp.zeros((head, line), f32), pg2, q_at[1] - split)
+    got_pg2 = scatter_rows(pg2, pgi2, "pg2")
+    second_path = projection(pg2, dwb2, dws2, dwc2, dwr2, wg2, "w2")
+    next(second_path)
+    next(first_path)
+    for copy in got_pg1:
+        copy.wait_recv()
+    n1g = dot(pgi1[0], whm[0, :, 0:split], 1, 1)
+    for g in range(1, GROUPS):
+        n1g = n1g + dot(pgi1[g], whm[g, :, 0:split], 1, 1)
+    next(second_path)
+    next(up_path)
+    next(out_path)
+    for copy in got_pg2:
+        copy.wait_recv()
+    for g in range(GROUPS):
+        n1g = n1g + dot(pgi2[g], whm[g, :, split : split + 4 * head], 1, 1)
+    normal = normal1[...]
+    vec[1:2, :] = column_sum(n1g)
+    vec[2:3, :] = column_sum(n1g * normal)
+    grad = normalise_back(n1g * (gain1 * (1.0 + scale1)), normal, spread1[...]) + middle_grad[...]
+    o_in[...] = grad
+    vec[0:1, :] = column_sum(grad * mcol[...])
+    vpl[chip] = vec[...]
+    i = ids("vp", 3)
+    got_vp = [send(vec, vpl.at[chip], i + k - 1, dev(k)) for k in (1, 2, 3)]
+    next(second_path)
+    next(first_path)
+    next(down_path)
+    for copy in got_vp:
+        copy.wait_recv()
+    vzs[z, 0:8] = (vpl[0, 0:8] + vpl[1, 0:8]) + (vpl[2, 0:8] + vpl[3, 0:8])
+    vzs[z, 8:16] = vpl[y, 8:16] + vpl[2 + y, 8:16]
+    iv = ids("vz", 3)
+    got_vz = [send(vzs.at[z], vzs.at[z], iv + k - 1, zdev(k)) for k in (1, 2, 3)]
+    next(first_path)
+    next(second_path)
+    next(out_path)
+    next(up_path)
+    for copy in got_vz:
+        copy.wait_recv()
+    vco[c] = (vzs[0] + vzs[1]) + (vzs[2] + vzs[3])
+    got_vc = send(vco.at[c], vco.at[c], ids("vc", 1), sib)
+    next(first_path)
+    next(out_path)
+    og[t] = wgt[...]
+    og1, og2, ogi = group_start(og, "og")
+    next(second_path)
+    got_vc.wait_recv()
+    sums = vco[0] + vco[1]
+    o_vec[0:1, :] = sums[0:1, :]
+    o_vec[1:2, :] = sums[2:3, :] * (1.0 + scale1)
+    o_vec[2:3, :] = sums[5:6, :] * (1.0 + scale2)
+    o_vec[3:4, :] = sums[7:8, :]
+    o_vec[4:5, :] = vco[c, 8:9, :]
+    o_vec[5:8, :] = jnp.zeros((3, width), f32)
+    o_vec[8:9, :] = sums[1:2, :]
+    o_vec[9:10, :] = sums[2:3, :] * gain1
+    o_vec[10:11, :] = sums[3:4, :]
+    o_vec[11:12, :] = sums[4:5, :]
+    o_vec[12:13, :] = sums[5:6, :] * gain2
+    o_vec[13:14, :] = sums[6:7, :]
+    o_vec[14:16, :] = jnp.zeros((2, width), f32)
+    next(down_path)
+    copies = [pltpu.make_async_copy(mgat.at[width : 2 * width], o_mlp.at[width : 2 * width], ls.at[0])]
+    copies[-1].start()
+    next(first_path)
+    copies.append(pltpu.make_async_copy(wg1, o_qkv1, ls.at[1]))
+    copies[-1].start()
+    og3 = group_pass(og, og2, ogi)
+    next(second_path)
+    next(up_path)
+    copies.append(pltpu.make_async_copy(mgat.at[0:width], o_mlp.at[0:width], ls.at[2]))
+    copies[-1].start()
+    next(second_path)
+    copies.append(pltpu.make_async_copy(wg2, o_qkv2, ls.at[3]))
+    copies[-1].start()
+    og1.wait_recv()
+    og3.wait_recv()
+    copies.append(pltpu.make_async_copy(og, o_ow, ls.at[4]))
+    copies[-1].start()
+    for copy in pending:
+        copy.wait_send()
+    for k in range(CHIPS):
+        remote(kvall.at[:, 0], kvall.at[:, 0], kdi + k, sib).wait_send()
+
+    def drain(i, carry):
+        remote(sbo.at[i], sbi.at[0, 0], sbx + (per - 1) * CHIPS + i, sib).wait_send()
+        return carry
+
+    lax.fori_loop(0, CHIPS, drain, 0)
+
+    def drain(i, carry):
+        remote(rso.at[i], rsi.at[0, 0], rsx + (per - 1) * 3 + i, sib).wait_send()
+        return carry
+
+    lax.fori_loop(0, 3, drain, 0)
+    for copy in copies:
+        copy.wait()
+
+
+def rope_constants(length, rows, head):
+    half = head // 2
+    inverse = np.exp(np.float32(-math.log(10000.0)) * np.arange(half, dtype=np.float32) / half)
+    angles = np.arange(length, dtype=np.float32)[:, None] * inverse.astype(np.float32)[None, :]
+    angles = np.tile(angles, (1, 4)).astype(np.float64)
+    shape = (length // rows, rows, 2 * head)
+    return (
+        jnp.asarray(np.cos(angles).astype(np.float32).reshape(shape)),
+        jnp.asarray(np.sin(angles).astype(np.float32).reshape(shape)),
+    )
+
+
+def fused_device(
+    seq_size,
+    tp_size,
+    tokens,
+    cotangent,
+    prefix_length,
+    mask_flags,
+    timestep,
+    mask_embed,
+    ln1_gain,
+    ln2_gain,
+    ada_weight,
+    ada_bias,
+    qkv_weight,
+    out_weight,
+    up_weight,
+    up_bias,
+    down_weight,
+    down_bias,
+):
+    rows, width = tokens.shape
+    head = width // HEADS
+    per = HEADS // GROUPS
+    gw = per * head
+    line = GROUPS * rows
+    packed = (per * 2 + 4) * head
+    shard = width // (2 * CHIPS)
+    cond = ada_weight.shape[0]
+    cosine, sine = rope_constants(rows * seq_size * tp_size, rows, head)
+    V = pltpu.VMEM
+    vmem = pl.BlockSpec(memory_space=pltpu.VMEM)
+    hbm = pl.BlockSpec(memory_space=pl.ANY)
+    parts = (6 * head, 4 * head)
+    outs = pl.pallas_call(
+        functools.partial(fused_kernel, tp_size),
+        out_shape=[
+            jax.ShapeDtypeStruct((rows, width), bf16),
+            jax.ShapeDtypeStruct((rows, width), f32),
+            jax.ShapeDtypeStruct((16, width), f32),
+            jax.ShapeDtypeStruct((GROUPS, CHIPS, 2, shard, parts[0]), bf16),
+            jax.ShapeDtypeStruct((GROUPS, CHIPS, 2, shard, parts[1]), bf16),
+            jax.ShapeDtypeStruct((tp_size, 2 * gw, width // 2), bf16),
+            jax.ShapeDtypeStruct((2 * width, width), bf16),
+        ],
+        in_specs=[pl.BlockSpec(memory_space=pltpu.SMEM)] * 2
+        + [vmem] * 9
+        + [hbm] * 4
+        + [vmem] * 3,
+        out_specs=[vmem] * 3 + [hbm] * 4,
+        scratch_shapes=[
+            V((8, width), f32),
+            V((rows, width), f32),
+            V((rows, width), f32),
+            V((rows, 1), f32),
+            V((rows, width), f32),
+            V((rows, 1), f32),
+            V((rows, width), f32),
+            V((rows, width), f32),
+            V((rows, 1), f32),
+            V((GROUPS, rows, width), bf16),
+            V((width, line), bf16),
+            V((GROUPS, width, packed), bf16),
+            V((GROUPS, rows, 2 * head), f32),
+            V((GROUPS, rows, 2 * head), f32),
+            V((per, 2 * CHIPS, line, 2 * head), bf16),
+            V((per, line, 2 * head), bf16),
+            V((per, 2 * CHIPS, line, line), bf16),
+            V((per, 2 * CHIPS, 1, line), f32),
+            V((per, 1, line), f32),
+            V((per, 1, line), f32),
+            V((per, 2 * head, line), f32),
+            V((per, 1, line), f32),
+            V((per, 1, line), f32),
+            V((GROUPS, gw, rows), bf16),
+            V((GROUPS, gw, rows), bf16),
+            V((tp_size, rows, width), bf16),
+            V((tp_size, rows, width), bf16),
+            V((tp_size, rows, width), bf16),
+            V((tp_size, rows, width), bf16),
+            V((tp_size, rows, width), f32),
+            V((2, rows, width), f32),
+            V((2, 2, rows, width), bf16),
+            V((2, 2, rows, width), bf16),
+            V((2, rows, width), bf16),
+            V((2, rows, width), bf16),
+            V((tp_size, rows, width), bf16),
+            V((tp_size, gw, rows), bf16),
+            V((GROUPS, gw, rows), bf16),
+            V((GROUPS, gw, rows), bf16),
+            V((per, 2 * head, line), bf16),
+            V((CHIPS, line, 2 * head), bf16),
+            V((per, CHIPS, line, 2 * head), bf16),
+            V((3, line, 2 * head), bf16),
+            V((per, 3, line, 2 * head), bf16),
+            V((per, line, 2 * head), f32),
+        ]
+        + [V((GROUPS, rows, n), bf16) for n in parts for _ in range(2)]
+        + [
+            V(shape, bf16)
+            for n in parts
+            for shape in (
+                (2, CHIPS, shard, n),
+                (CHIPS, shard, n),
+                (CHIPS, shard, n),
+                (3, shard, n),
+                (GROUPS, CHIPS, 2, shard, n),
+            )
+        ]
+        + [
+            V((2 * gw, width // 2), bf16),
+            V((gw, width // 2), bf16),
+            V((3, gw // GROUPS, width // 2), bf16),
+            V((2 * gw, width // 2), bf16),
+            V((tp_size, 2 * gw, width // 2), bf16),
+            V((2 * width, width), bf16),
+            V((width, width), bf16),
+            V((2, 3, shard, width), bf16),
+            V((2 * width, width), bf16),
+            V((16, width), f32),
+            V((CHIPS, 16, width), f32),
+            V((GROUPS, 16, width), f32),
+            V((2, 16, width), f32),
+            pltpu.SemaphoreType.DMA((160,)),
+            pltpu.SemaphoreType.DMA((160,)),
+            pltpu.SemaphoreType.DMA((17,)),
+        ],
+        compiler_params=pltpu.CompilerParams(
+            collective_id=0, has_side_effects=True, vmem_limit_bytes=VMEM_LIMIT
+        ),
+    )(
+        prefix_length,
+        timestep,
+        mask_flags,
+        mask_embed,
+        ln1_gain,
+        ln2_gain,
+        up_bias,
+        down_bias,
+        ada_bias,
+        tokens,
+        cotangent,
+        cosine,
+        sine,
+        ada_weight,
+        qkv_weight,
+        out_weight,
+        up_weight,
+        down_weight,
+    )
+    output, input_grad, sums, first, second, out_parts, mlp_parts = outs
+    steps = 2 * CHIPS
+    vector = jax.ShapeDtypeStruct((width,), f32)
+    whole = pl.BlockSpec((width,), lambda n: (0,))
+
+    def some(*shape):
+        return jax.ShapeDtypeStruct(shape, f32)
+
+    def rows_of(count, columns, skip=0):
+        return pl.BlockSpec((count, columns), lambda n: (n + skip, 0))
+
+    return pl.pallas_call(
+        functools.partial(finish_kernel, per, head),
+        grid=(steps,),
+        out_shape=[
+            jax.ShapeDtypeStruct((rows, width), bf16),
+            some(rows, width),
+            vector,
+            vector,
+            vector,
+            some(cond, 6 * width),
+            some(6 * width),
+            some(width, 3 * width),
+            some(width, width),
+            some(width, width),
+            vector,
+            some(width, width),
+            vector,
+        ],
+        in_specs=[
+            pl.BlockSpec(memory_space=pltpu.SMEM),
+            pl.BlockSpec((16, width), lambda n: (0, 0)),
+            rows_of(rows // steps, width),
+            rows_of(rows // steps, width),
+            pl.BlockSpec((GROUPS, 1, shard, parts[0]), lambda n: (0, n, 0, 0)),
+            pl.BlockSpec((GROUPS, 1, shard, parts[1]), lambda n: (0, n, 0, 0)),
+            pl.BlockSpec((1, 2, shard, width // 2), lambda n: (n // 2, 0, n % 2, 0)),
+            rows_of(shard, width),
+            rows_of(shard, width, steps),
+        ],
+        out_specs=[
+            rows_of(rows // steps, width),
+            rows_of(rows // steps, width),
+            whole,
+            whole,
+            whole,
+            rows_of(cond // steps, 6 * width),
+            pl.BlockSpec((6 * width,), lambda n: (0,)),
+            rows_of(shard, 3 * width),
+            rows_of(shard, width),
+            rows_of(shard, width),
+            whole,
+            rows_of(shard, width),
+            whole,
+        ],
+    )(
+        timestep,
+        sums,
+        output,
+        input_grad,
+        first.reshape(GROUPS, steps, shard, parts[0]),
+        second.reshape(GROUPS, steps, shard, parts[1]),
+        out_parts.reshape(tp_size, 2, gw, width // 2),
+        mlp_parts,
+        mlp_parts,
+    )
+
+
 def solution(mesh):
+    seq_size, tp_size = mesh.shape["seq"], mesh.shape["tp"]
+    small = seq_size == 2 * GROUPS and tp_size == CHIPS
     in_specs = (
         P(("seq", "tp"), None),
         P(("seq", "tp"), None),
@@ -394,5 +1449,6 @@
         P(),
     )
     return jax.shard_map(
-        per_device, mesh=mesh, in_specs=in_specs, out_specs=out_specs, check_vma=False
-    )
+        functools.partial(fused_device, seq_size, tp_size) if small else per_device,
+        mesh=mesh, in_specs=in_specs, out_specs=out_specs, check_vma=False
+    )

time: 743 us -> 215 us (0.29); the launches traced: 729 us -> 214 us
  waiting for transfers between devices: 259 us -> 0 us
  Pallas kernels: 0 us -> 212 us
  blocking collectives: 171 us -> 0 us
  matrix products: 147 us -> 0 us
  local copies, waits for them, and re-layouts: 73.6 us -> 0 us
  other arithmetic: 31.7 us -> 0 us
  starting transfers between devices: 30.1 us -> 0 us
  between operations: 16.5 us -> 2.13 us
    pallas_call x0 -> x2, Pallas kernels: none -> 212 us  [the longest x1 201 us: fused_device(): pl.pallas_call(functools.partial(fused_kernel, tp_size), out_shape=[jax.S...]
    psum x2 -> x0, waiting for transfers between devices: 156 us -> none  [the longest x1 156 us: per_device(): lax.psum((qkv_weight_grad, out_weight_grad, modulation_grad, gain_one_gra...]
    dot_general x27 -> x0, matrix products: 147 us -> none  [the longest x2 21.1 us: query_update(): jnp.einsum('hqk,khd->qhd', score_grad, key_block, preferred_element_type=...]
    all_gather x4 -> x0, blocking collectives: 83.2 us -> none  [the longest x1 32.6 us: per_device(): lax.all_gather(delta_rows, 'seq', axis=0, tiled=True)]
    all_gather x4 -> x0, waiting for transfers between devices: 63.2 us -> none  [the longest x1 46.1 us: per_device(): every_value = lax.all_gather(value_rows, 'seq', axis=0, tiled=True)]
    psum x2 -> x0, blocking collectives: 62.4 us -> none  [the longest x1 39.8 us: per_device(): lax.psum((qkv_weight_grad, out_weight_grad, modulation_grad, gain_one_gra...]
    reduce_scatter x2 -> x0, waiting for transfers between devices: 36.2 us -> none  [the longest x1 21.4 us: per_device(): lax.psum_scatter(jnp.dot(active, down_weight, preferred_element_type=jnp....]
    all_to_all x5 -> x0, starting transfers between devices: 29.5 us -> none  [the longest x4 25.5 us: to_rows(): return lax.all_to_all(rows, 'tp', split_axis=0, concat_axis=1, tiled=True)]
  transfers between devices with their start and end apart: 13 -> 0, of which waited for: 8 -> 0; matrix products, arithmetic and copies ran while one was open for 22% -> 0% of each run, Pallas kernels for 0% -> 0%
where the time goes in v2:
time: 215 us; the launch traced here: 214 us
  Pallas kernels  212 us (99%)
    pallas_call x1, Pallas kernels, fused_device(): pl.pallas_call(functools.partial(fused_kernel, tp_size), out_shape=[jax.S...  201 us
    pallas_call x1, Pallas kernels, fused_device(): pl.pallas_call(functools.partial(finish_kernel, per, head), grid=(steps,)...  11.1 us

profile of v2, /device:TPU:0, one launch (start us, length us, event | category | flops | bytes accessed | tf_op | source)
XLA Modules:
  0.0 214.1 jit_solution(1088642820223197710)
XLA Ops:
  1.9 200.9 %shard_map.273 = (bf16[128,768]{1,0:T(8,128)(2,1)}, f32[128,768]{1,0:T(8,128)}, f32[16,768]{1,0:T(8,128)}, bf16[4,4,2,96,384]{4,3,2,1,0:T(8,128)(2,1)}, bf16[4,4...) custom-call(s32[1]{0:T(128)S(6)} %copy.31.prefix_ref, ...), custom_call_target="tpu_custom_call" | custom-call | tf_op jit(solution)/shard_map/pallas_call | solution.py:1231
  202.9 11.1 %shard_map.274 = (bf16[128,768]{1,0:T(8,128)(2,1)}, f32[128,768]{1,0:T(8,128)}, f32[768]{0:T(1024)}, f32[768]{0:T(1024)}, f32[768]{0:T(1024)}, /*index=5*/f32[12...) custom-call(s32[1]{0:T(128)S(6)} %copy.32.timestep_ref, ...), custom_call_target="tpu_custom_call" | custom-call | tf_op jit(solution)/shard_map/pallas_call | solution.py:1358

commit v3 on v2

--- a/solution.py
+++ b/solution.py
@@ -485,9 +485,9 @@
     sin_hbm,
     ada_hbm,
     qkv_hbm,
-    out_w,
-    up_w,
-    down_w,
+    out_hbm,
+    up_hbm,
+    down_hbm,
     o_out,
     o_in,
     o_vec,
@@ -495,6 +495,9 @@
     o_qkv2,
     o_ow,
     o_mlp,
+    out_w,
+    up_w,
+    down_w,
     mod,
     start,
     normal1,
@@ -505,7 +508,9 @@
     middle_grad,
     mcol,
     nl,
-    nt,
+    kvo,
+    qo,
+    qi,
     whm,
     cosb,
     sinb,
@@ -539,6 +544,8 @@
     sbi,
     rso,
     rsi,
+    rsx_out,
+    rsx_in,
     dkv,
     pg1,
     pgi1,
@@ -645,19 +652,23 @@
         for i in range(6)
     ]
     stage = [mbuf.at[0:width], mbuf.at[width : 2 * width], mgat.at[0:width]]
-    raw = [local(qkv_hbm.at[:, i * width : (i + 1) * width], stage[i], i) for i in range(3)]
+    raw = []
     for zb in range(GROUPS):
         block = (zb * 2 + x) * tp_size + t
-        raw.append(local(cos_hbm.at[block], cosb.at[zb], 3 + zb))
-        raw.append(local(sin_hbm.at[block], sinb.at[zb], 7 + zb))
-
+        raw.append(local(cos_hbm.at[block], cosb.at[zb], zb))
+        raw.append(local(sin_hbm.at[block], sinb.at[zb], 4 + zb))
+    raw += [local(qkv_hbm.at[:, i * width : (i + 1) * width], stage[i], 8 + i) for i in range(3)]
+    loads = zip((down_hbm, out_hbm, up_hbm), (down_w, out_w, up_w))
+    weights = [local(src, dst, 17 + i) for i, (src, dst) in enumerate(loads)]
     act = activation_of(timestep_ref[0], 0, cond, cond)
-    for i in range(6):
-        ada[i].wait()
-        part = msi[i * cond : (i + 1) * cond, :].astype(f32)
-        mod[i : i + 1, :] = column_sum(part * act) + row_of(ada_b_ref, i, width)
-    shift1, scale1, gate1 = mod[0:1, :], mod[1:2, :], mod[2:3, :]
-    shift2, scale2, gate2 = mod[3:4, :], mod[4:5, :], mod[5:6, :]
+    def modulate_rows(first, last):
+        for i in range(first, last):
+            ada[i].wait()
+            part = msi[i * cond : (i + 1) * cond, :].astype(f32)
+            mod[i : i + 1, :] = column_sum(part * act) + row_of(ada_b_ref, i, width)
+
+    modulate_rows(0, 2)
+    shift1, scale1 = mod[0:1, :], mod[1:2, :]
     embed, gain1, gain2, up_b, down_b = (
         row_of(ref, 0, width) for ref in (embed_ref, gain1_ref, gain2_ref, up_b_ref, down_b_ref)
     )
@@ -669,11 +680,8 @@
     normal1[...] = normal
     spread1[...] = spread
     nl[z] = (normal * (gain1 * (1.0 + scale1)) + shift1).astype(bf16)
-    rg[t] = (cot_ref[...].astype(f32) * gate2).astype(bf16)
 
     pl.semaphore_wait(barrier, len(peers))
-    zi = ids("nl", 3)
-    got_nl = [send(nl.at[z], nl.at[z], zi + k - 1, zdev(k)) for k in (1, 2, 3)]
 
     def group_start(buffer, name):
         i = ids(name, 3)
@@ -686,10 +694,59 @@
         other = (1 - y) * 2 + c
         return send(buffer.at[other], buffer.at[other], i, sib)
 
-    rg1, rg2, rgi = group_start(rg, "rg")
 
     for copy in raw:
         copy.wait()
+    lane = lax.broadcasted_iota(jnp.int32, (rows, 2 * head), 1)
+    low_half = lane < head
+    first = (lane % head) < head // 2
+    half = head // 2
+
+    def turn(tile, cosine, sine):
+        ahead = jnp.where(first, -pltpu.roll(tile, 2 * head - half, 1), pltpu.roll(tile, half, 1))
+        return tile * cosine + ahead * sine
+
+    def turn_back(tile, cosine, sine):
+        moved = tile * sine
+        behind = jnp.where(first, pltpu.roll(moved, 2 * head - half, 1), -pltpu.roll(moved, half, 1))
+        return tile * cosine + behind
+
+    kvi = ids("kv", 12)
+    scale = head ** (-0.5)
+    cosine, sine = cosb[z], sinb[z]
+    thirds = [dot(nl[z], ref[...], 1, 0) for ref in stage]
+
+    def of_head(third, n):
+        return thirds[third][:, n * head : (n + 1) * head]
+
+    for g in range(GROUPS):
+        for h in range(per):
+            n = g * per + h
+            tile = jnp.concatenate([of_head(1, n), of_head(2, n)], axis=1)
+            kvo[g, h] = jnp.where(low_half, turn(tile, cosine, sine), tile).astype(bf16)
+    here = pl.ds(z * rows, rows)
+    zi = ids("kvz", 3)
+    got_kv = []
+    for k in (1, 2, 3):
+        there = kvall.at[:, p, here, :]
+        got_kv.append(send(kvo.at[(z + k) % 4], there, zi + k - 1, zdev(k)))
+    kvall[:, p, here, :] = kvo[z]
+
+    def over_plane(k):
+        src = kvall.at[:, p, pl.ds(zfrom(k) * rows, rows), :]
+        for kk in (1, 2, 3):
+            send(src, src, kvi + (kk - 1) * 4 + k, dev(kk))
+
+    over_plane(0)
+    for g in range(GROUPS):
+        n = g * per
+        tile = turn(thirds[0][:, n * head : (n + 2) * head], cosine, sine) * scale
+        qo[g, 0] = tile.astype(bf16)
+        tile = jnp.concatenate([of_head(0, n + 2), jnp.zeros((rows, head), f32)], axis=1)
+        qo[g, 1] = (turn(tile, cosine, sine) * scale).astype(bf16)
+    i = ids("q", 3)
+    got_q = [send(qo.at[(z + k) % 4], qi.at[z], i + k - 1, zdev(k)) for k in (1, 2, 3)]
+    qi[z] = qo[z]
     for g in range(GROUPS):
         for h in range(per):
             a = g * gw + h * head
@@ -700,42 +757,26 @@
         tile = [mbuf[0:width, a + 2 * head : a + 3 * head], jnp.zeros((width, head), bf16)]
         whm[g, :, q_at[1] : q_at[1] + 2 * head] = jnp.concatenate(tile, axis=1)
 
-    lane = lax.broadcasted_iota(jnp.int32, (rows, 2 * head), 1)
-    low_half = lane < head
-    first = (lane % head) < head // 2
-    half = head // 2
-
-    def turn(tile, cosine, sine):
-        ahead = jnp.where(first, -pltpu.roll(tile, 2 * head - half, 1), pltpu.roll(tile, half, 1))
-        return tile * cosine + ahead * sine
-
-    def turn_back(tile, cosine, sine):
-        moved = tile * sine
-        behind = jnp.where(first, pltpu.roll(moved, 2 * head - half, 1), -pltpu.roll(moved, half, 1))
-        return tile * cosine + behind
-
-    kvi = ids("kv", 12)
-    scale = head ** (-0.5)
-    for k in range(GROUPS):
-        zb = zfrom(k)
-        if k:
-            got_nl[k - 1].wait_recv()
-        proj = dot(nl[zb], whm[z], 1, 0)
-        cosine, sine = cosb[zb], sinb[zb]
-        here = pl.ds(zb * rows, rows)
-        for h in range(per):
-            tile = proj[:, kv_at[h] : kv_at[h] + 2 * head]
-            kvall[h, p, here, :] = jnp.where(low_half, turn(tile, cosine, sine), tile).astype(bf16)
-        for kk in (1, 2, 3):
-            src = kvall.at[:, p, here, :]
-            send(src, src, kvi + (kk - 1) * 4 + k, dev(kk))
-        for i in range(2):
-            tile = turn(proj[:, q_at[i] : q_at[i] + 2 * head], cosine, sine) * scale
-            qd[2 * i, here, :] = jnp.where(low_half, tile, 0.0).astype(bf16)
-            if i == 0:
-                qd[1, here, :] = jnp.where(low_half, pltpu.roll(tile, head, 1), 0.0).astype(bf16)
+    modulate_rows(2, 6)
+    gate1, shift2 = mod[2:3, :], mod[3:4, :]
+    scale2, gate2 = mod[4:5, :], mod[5:6, :]
+    rg[t] = (cot_ref[...].astype(f32) * gate2).astype(bf16)
+    rg1, rg2, rgi = group_start(rg, "rg")
+    for k in (1, 2, 3):
+        got_kv[k - 1].wait_recv()
+        over_plane(k)
+    i = ids("nl", 3)
+    got_nl = [send(nl.at[z], nl.at[z], i + k - 1, zdev(k)) for k in (1, 2, 3)]
     kdi = ids("kvd", 4)
     remote(kvall.at[:, p], kvall.at[:, p], kdi, sib).start()
+    for copy in got_q:
+        copy.wait_recv()
+    for zb in range(GROUPS):
+        at = slice(zb * rows, (zb + 1) * rows)
+        pair, last = qi[zb, 0].astype(f32), qi[zb, 1].astype(f32)
+        qd[0, at, :] = jnp.where(low_half, pair, 0.0).astype(bf16)
+        qd[1, at, :] = jnp.where(low_half, pltpu.roll(pair, head, 1), 0.0).astype(bf16)
+        qd[2, at, :] = jnp.where(low_half, last, 0.0).astype(bf16)
 
     mrun[...] = jnp.full_like(mrun, floor_value)
     lrun[...] = jnp.zeros_like(lrun)
@@ -784,13 +825,15 @@
     got_mix = [send(mtb.at[(z + k) % 4], mi.at[z], i + k - 1, zdev(k)) for k in (1, 2, 3)]
     mi[z] = mtb[z]
     rg3 = group_pass(rg, rg2, rgi)
-    nt[...] = nl[...].reshape(line, width).T
     rg1.wait_recv()
     rg3.wait_recv()
+    weights[0].wait()
     for tb in range(tp_size):
         ag[tb] = dot(rg[tb], down_w[...], 1, 1)
     for copy in got_mix:
         copy.wait_recv()
+    weights[1].wait()
+    weights[2].wait()
     total = dot(mi[0], out_w[0:gw, :], 0, 0)
     for g in range(1, GROUPS):
         total = total + dot(mi[g], out_w[g * gw : (g + 1) * gw, :], 0, 0)
@@ -858,7 +901,7 @@
     )
     half_rows = width // 2
 
-    def exchange(part, buffer, incoming, parts, gathered, base, count, name):
+    def exchange(buffer, incoming, parts, gathered, base, count, name):
         near, own = count // 2, count // 2 // GROUPS
         i = ids(name, 8)
         src = buffer.at[pl.ds(base + (1 - x) * near, near)]
@@ -867,19 +910,31 @@
         got.wait_recv()
         mine = buffer[pl.ds(base + x * near, near), :].astype(f32) + incoming[...].astype(f32)
         incoming[...] = mine.astype(bf16)
+        beside = ((z + 1 - 2 * (z % 2)) * 2 + x, t)
         got = []
-        for k in (1, 2, 3):
-            src = incoming.at[pl.ds(((z + k) % 4) * own, own)]
-            got.append(send(src, parts.at[k - 1], i + k, zdev(k)))
+        for n in range(2):
+            src = incoming.at[pl.ds((n * 2 + 1 - z % 2) * own, own)]
+            got.append(send(src, parts.at[n], i + 1 + n, beside))
         yield
-        for copy in got:
-            copy.wait_recv()
-        mine = incoming[pl.ds(z * own, own), :].astype(f32)
-        for k in range(3):
-            mine = mine + parts[k].astype(f32)
-        src = gathered.at[pl.ds(base + x * near + z * own, own)]
+        for n in range(2):
+            got[n].wait_recv()
+            src = incoming.at[pl.ds((n * 2 + z % 2) * own, own)]
+            src[...] = (src[...].astype(f32) + parts[n].astype(f32)).astype(bf16)
+        src = incoming.at[pl.ds(((z + 2) % 4) * own, own)]
+        got = send(src, parts.at[2], i + 3, zdev(2))
+        yield
+        got.wait_recv()
+        mine = incoming[pl.ds(z * own, own), :].astype(f32) + parts[2].astype(f32)
+
+        def place(d):
+            return gathered.at[pl.ds(base + x * near + d * own, own)]
+
+        src = place(z)
         src[...] = mine.astype(bf16)
-        got = [send(src, src, i + 3 + k, zdev(k)) for k in (1, 2, 3)]
+        got = send(src, src, i + 4, zdev(2))
+        yield
+        got.wait_recv()
+        got = [send(place(d), place(d), i + 5 + n, beside) for n, d in enumerate((z, (z + 2) % 4))]
         yield
         for copy in got:
             copy.wait_recv()
@@ -891,7 +946,7 @@
 
     def exchange_of(m):
         side = pl.ds(m * half_rows, half_rows)
-        return exchange(m, mbuf, msi.at[side], mz.at[m], mgat, m * width, width, f"m{m}")
+        return exchange(mbuf, msi.at[side], mz.at[m], mgat, m * width, width, f"m{m}")
 
     def matrix(left, right):
         return dot(left[...].reshape(line, width), right[...].reshape(line, width), 0, 0)
@@ -938,7 +993,7 @@
     dq = ot
     dq[...] = jnp.zeros_like(dq)
     sbx = ids("sb", 12)
-    rsx = ids("rs", 9)
+    rsi_at = ids("rs", 9)
 
     def backward(i, carry):
         h, r = i // (2 * CHIPS), i % (2 * CHIPS)
@@ -972,25 +1027,44 @@
             def _():
                 dkv[h] = both
 
-            @pl.when((k > 0) & (h > 0))
+            final = h // (per - 1)
+
+            @pl.when(k == 2)
             def _():
-                remote(rso.at[k - 1], rsi.at[h, k - 1], rsx + (h - 1) * 3 + k - 1, sib).wait_send()
-
-            @pl.when(k > 0)
+                rsx_out[h] = both.astype(bf16)
+
+            @pl.when((k == 2) & (final == 1))
             def _():
-                rso[k - 1] = both.astype(bf16)
-                remote(rso.at[k - 1], rsi.at[h, k - 1], rsx + h * 3 + k - 1, dev(k)).start()
+                remote(rsx_out.at[h], rsx_in.at[h], rsi_at + h * 3 + 2, dev(2)).start()
+
+            odd = k // 2
+
+            @pl.when((k % 2 == 1) & (h > 0))
+            def _():
+                remote(rso.at[odd], rsi.at[h, odd], rsi_at + (h - 1) * 3 + odd, sib).wait_send()
+
+            @pl.when(k % 2 == 1)
+            def _():
+                rso[odd] = both.astype(bf16)
+                remote(rso.at[odd], rsi.at[h, odd], rsi_at + h * 3 + odd, dev(1 + 2 * odd * final)).start()
 
         return carry
 
     def backward_from(first, last):
         lax.fori_loop(first, last, backward, 0)
 
+    def relay(h):
+        remote(rso.at[1], rsi.at[h, 1], rsi_at + h * 3 + 1, sib).wait_recv()
+        rsx_out[h] = (rsx_out[h].astype(f32) + rsi[h, 1].astype(f32)).astype(bf16)
+        return send(rsx_out.at[h], rsx_in.at[h], rsi_at + h * 3 + 2, dev(2))
+
     def keys_back(h, out, b):
-        total = dkv[h]
-        for k in range(3):
-            remote(rso.at[k], rsi.at[h, k], rsx + h * 3 + k, sib).wait_recv()
-            total = total + rsi[h, k].astype(f32)
+        remote(rso.at[0], rsi.at[h, 0], rsi_at + h * 3, sib).wait_recv()
+        across[h].wait_recv()
+        total = dkv[h] + (rsi[h, 0].astype(f32) + rsx_in[h].astype(f32))
+        if h == per - 1:
+            remote(rso.at[1], rsi.at[h, 1], rsi_at + h * 3 + 1, sib).wait_recv()
+            total = total + rsi[h, 1].astype(f32)
         for zb in range(GROUPS):
             tile = total[zb * rows : (zb + 1) * rows, :]
             back = jnp.where(low_half, turn_back(tile, cosb[zb], sinb[zb]), tile)
@@ -1009,7 +1083,7 @@
         return got
 
     def projection(out, mine, other, summed, incoming, gathered, name):
-        grad = dot(nt[...], out[...].reshape(line, out.shape[2]), 1, 0)
+        grad = dot(nl[...].reshape(line, width), out[...].reshape(line, out.shape[2]), 0, 0)
         for n in range(2 * CHIPS):
             mine[n % 2, n // 2] = grad[n * shard : (n + 1) * shard, :].astype(bf16)
         i = ids(name, 13)
@@ -1051,8 +1125,9 @@
             copy.wait_recv()
         yield
 
+    across = {}
+    backward_from(0, 8)
     next(down_path)
-    backward_from(0, 8)
     bg1.wait_recv()
     bg3.wait_recv()
     for copy in got_mig:
@@ -1063,38 +1138,49 @@
     wide = width // 2
     wbuf[0:gw, :] = grad[:, 0:wide].astype(bf16)
     wbuf[gw : 2 * gw, :] = grad[:, wide:width].astype(bf16)
-    out_path = exchange(2, wbuf, wsi, wz, wgt, 0, 2 * gw, "wo")
+    out_path = exchange(wbuf, wsi, wz, wgt, 0, 2 * gw, "wo")
     next(out_path)
     result = finish_result() + down_b
     o_out[...] = (start[...] + gate2 * result).astype(bf16)
     vec[6:7, :] = column_sum(cot_ref[...].astype(f32) * result)
     backward_from(8, 16)
+    across[0] = relay(0)
+    next(down_path)
     next(up_path)
     backward_from(16, 20)
+    across[1] = relay(1)
+    backward_from(20, 24)
+    across[2] = remote(rsx_out.at[per - 1], rsx_in.at[per - 1], rsi_at + per * 3 - 1, dev(2))
+    pending.append(across[2])
+    next(out_path)
+    next(down_path)
+    for copy in got_nl:
+        copy.wait_recv()
     keys_back(0, pg1, kv_at[0])
     keys_back(1, pg1, kv_at[1])
     queries_back(dq[0, 0:head, :], dq[1, 0:head, :], pg1, q_at[0])
     got_pg1 = scatter_rows(pg1, pgi1, "pg1")
     first_path = projection(pg1, dwb1, dws1, dwc1, dwr1, wg1, "w1")
     next(first_path)
-    next(down_path)
-    backward_from(20, 24)
-    next(first_path)
-    next(out_path)
     keys_back(2, pg2, kv_at[2] - split)
     queries_back(dq[2, 0:head, :], jnp.zeros((head, line), f32), pg2, q_at[1] - split)
     got_pg2 = scatter_rows(pg2, pgi2, "pg2")
     second_path = projection(pg2, dwb2, dws2, dwc2, dwr2, wg2, "w2")
     next(second_path)
     next(first_path)
+    next(up_path)
+    next(out_path)
+    next(second_path)
+    next(first_path)
+    next(down_path)
+    next(second_path)
+    next(up_path)
+    next(out_path)
     for copy in got_pg1:
         copy.wait_recv()
     n1g = dot(pgi1[0], whm[0, :, 0:split], 1, 1)
     for g in range(1, GROUPS):
         n1g = n1g + dot(pgi1[g], whm[g, :, 0:split], 1, 1)
-    next(second_path)
-    next(up_path)
-    next(out_path)
     for copy in got_pg2:
         copy.wait_recv()
     for g in range(GROUPS):
@@ -1108,27 +1194,29 @@
     vpl[chip] = vec[...]
     i = ids("vp", 3)
     got_vp = [send(vec, vpl.at[chip], i + k - 1, dev(k)) for k in (1, 2, 3)]
-    next(second_path)
     next(first_path)
     next(down_path)
+    next(out_path)
+    next(second_path)
     for copy in got_vp:
         copy.wait_recv()
     vzs[z, 0:8] = (vpl[0, 0:8] + vpl[1, 0:8]) + (vpl[2, 0:8] + vpl[3, 0:8])
     vzs[z, 8:16] = vpl[y, 8:16] + vpl[2 + y, 8:16]
     iv = ids("vz", 3)
     got_vz = [send(vzs.at[z], vzs.at[z], iv + k - 1, zdev(k)) for k in (1, 2, 3)]
+    next(up_path)
+    next(out_path)
     next(first_path)
     next(second_path)
-    next(out_path)
-    next(up_path)
     for copy in got_vz:
         copy.wait_recv()
     vco[c] = (vzs[0] + vzs[1]) + (vzs[2] + vzs[3])
     got_vc = send(vco.at[c], vco.at[c], ids("vc", 1), sib)
-    next(first_path)
     next(out_path)
     og[t] = wgt[...]
     og1, og2, ogi = group_start(og, "og")
+    next(up_path)
+    next(first_path)
     next(second_path)
     got_vc.wait_recv()
     sums = vco[0] + vco[1]
@@ -1145,24 +1233,24 @@
     o_vec[12:13, :] = sums[5:6, :] * gain2
     o_vec[13:14, :] = sums[6:7, :]
     o_vec[14:16, :] = jnp.zeros((2, width), f32)
+    og3 = group_pass(og, og2, ogi)
+    copies = []
+
+    def write(src, dst):
+        copies.append(pltpu.make_async_copy(src, dst, ls.at[len(copies)]))
+        copies[-1].start()
+
     next(down_path)
-    copies = [pltpu.make_async_copy(mgat.at[width : 2 * width], o_mlp.at[width : 2 * width], ls.at[0])]
-    copies[-1].start()
+    write(mgat.at[width : 2 * width], o_mlp.at[width : 2 * width])
     next(first_path)
-    copies.append(pltpu.make_async_copy(wg1, o_qkv1, ls.at[1]))
-    copies[-1].start()
-    og3 = group_pass(og, og2, ogi)
+    write(wg1, o_qkv1)
     next(second_path)
-    next(up_path)
-    copies.append(pltpu.make_async_copy(mgat.at[0:width], o_mlp.at[0:width], ls.at[2]))
-    copies[-1].start()
-    next(second_path)
-    copies.append(pltpu.make_async_copy(wg2, o_qkv2, ls.at[3]))
-    copies[-1].start()
+    write(wg2, o_qkv2)
     og1.wait_recv()
     og3.wait_recv()
-    copies.append(pltpu.make_async_copy(og, o_ow, ls.at[4]))
-    copies[-1].start()
+    write(og, o_ow)
+    next(up_path)
+    write(mgat.at[0:width], o_mlp.at[0:width])
     for copy in pending:
         copy.wait_send()
     for k in range(CHIPS):
@@ -1175,10 +1263,10 @@
     lax.fori_loop(0, CHIPS, drain, 0)
 
     def drain(i, carry):
-        remote(rso.at[i], rsi.at[0, 0], rsx + (per - 1) * 3 + i, sib).wait_send()
+        remote(rso.at[i], rsi.at[0, 0], rsi_at + (per - 1) * 3 + i, sib).wait_send()
         return carry
 
-    lax.fori_loop(0, 3, drain, 0)
+    lax.fori_loop(0, 2, drain, 0)
     for copy in copies:
         copy.wait()
 
@@ -1241,10 +1329,12 @@
         ],
         in_specs=[pl.BlockSpec(memory_space=pltpu.SMEM)] * 2
         + [vmem] * 9
-        + [hbm] * 4
-        + [vmem] * 3,
+        + [hbm] * 7,
         out_specs=[vmem] * 3 + [hbm] * 4,
         scratch_shapes=[
+            V((width, width), bf16),
+            V((width, width), bf16),
+            V((width, width), bf16),
             V((8, width), f32),
             V((rows, width), f32),
             V((rows, width), f32),
@@ -1255,7 +1345,9 @@
             V((rows, width), f32),
             V((rows, 1), f32),
             V((GROUPS, rows, width), bf16),
-            V((width, line), bf16),
+            V((GROUPS, per, rows, 2 * head), bf16),
+            V((GROUPS, 2, rows, 2 * head), bf16),
+            V((GROUPS, 2, rows, 2 * head), bf16),
             V((GROUPS, width, packed), bf16),
             V((GROUPS, rows, 2 * head), f32),
             V((GROUPS, rows, 2 * head), f32),
@@ -1287,8 +1379,10 @@
             V((per, 2 * head, line), bf16),
             V((CHIPS, line, 2 * head), bf16),
             V((per, CHIPS, line, 2 * head), bf16),
-            V((3, line, 2 * head), bf16),
-            V((per, 3, line, 2 * head), bf16),
+            V((2, line, 2 * head), bf16),
+            V((per, 2, line, 2 * head), bf16),
+            V((per, line, 2 * head), bf16),
+            V((per, line, 2 * head), bf16),
             V((per, line, 2 * head), f32),
         ]
         + [V((GROUPS, rows, n), bf16) for n in parts for _ in range(2)]
@@ -1319,7 +1413,7 @@
             V((2, 16, width), f32),
             pltpu.SemaphoreType.DMA((160,)),
             pltpu.SemaphoreType.DMA((160,)),
-            pltpu.SemaphoreType.DMA((17,)),
+            pltpu.SemaphoreType.DMA((20,)),
         ],
         compiler_params=pltpu.CompilerParams(
             collective_id=0, has_side_effects=True, vmem_limit_bytes=VMEM_LIMIT

time: 215 us -> 200 us (0.930)
  Pallas kernels: 212 us -> 197 us
    pallas_call x1, Pallas kernels: 201 us -> 186 us  [fused_device(): pl.pallas_call(functools.partial(fused_kernel, tp_size), out_shape=[jax.S...]
where the time goes in v3:
time: 200 us; the launch traced here: 199 us
  Pallas kernels  197 us (98%)
  between operations  2.13 us (1%)
    pallas_call x1, Pallas kernels, fused_device(): pl.pallas_call(functools.partial(fused_kernel, tp_size), out_shape=[jax.S...  186 us
    pallas_call x1, Pallas kernels, fused_device(): pl.pallas_call(functools.partial(finish_kernel, per, head), grid=(steps,)...  11.1 us

profile of v3, /device:TPU:0, one launch (start us, length us, event | category | flops | bytes accessed | tf_op | source)
XLA Modules:
  0.0 199.3 jit_solution(13230548534306108199)
XLA Ops:
  1.9 186.1 %shard_map.273 = (bf16[128,768]{1,0:T(8,128)(2,1)}, f32[128,768]{1,0:T(8,128)}, f32[16,768]{1,0:T(8,128)}, bf16[4,4,2,96,384]{4,3,2,1,0:T(8,128)(2,1)}, bf16[4,4...) custom-call(s32[1]{0:T(128)S(6)} %copy.31.prefix_ref, ...), custom_call_target="tpu_custom_call" | custom-call | tf_op jit(solution)/shard_map/pallas_call | solution.py:1319
  188.0 11.1 %shard_map.274 = (bf16[128,768]{1,0:T(8,128)(2,1)}, f32[128,768]{1,0:T(8,128)}, f32[768]{0:T(1024)}, f32[768]{0:T(1024)}, f32[768]{0:T(1024)}, /*index=5*/f32[12...) custom-call(s32[1]{0:T(128)S(6)} %copy.32.timestep_ref, ...), custom_call_target="tpu_custom_call" | custom-call | tf_op jit(solution)/shard_map/pallas_call | solution.py:1452

commit v4 on v3

--- a/solution.py
+++ b/solution.py
@@ -363,6 +363,25 @@
     )
 
 
+ORDER = (
+    "d1_dw d2_dw ln2b u1_dw",
+    "d1_1 u2_dw res bgp",
+    "d2_1 d1_2 L1 u1_1",
+    "d2_2 d1_3 wo L2",
+    "u1_2 o_1 d2_3 rel0",
+    "L3a rel1 o_2 d1_4",
+    "u1_3 L3b o_3 por1",
+    "o_4 w1_a u2_1 por2",
+    "w2_a o_5 w2_b d1_5",
+    "resfin u2_2 u1_4 o_end",
+    "w1_b og n1g w2_c",
+    "d2_4 u1_5 u2_3 w2_d",
+    "w1_c v1 u2_4 d2_5",
+    "og2 d1_end w2_e w1_d",
+    "og3 w2_end u2_5 v2",
+    "v3 w1_e d2_end u1_end",
+    "w1_end u2_end",
+)
 VMEM_LIMIT = 63 * 2**20
 GROUPS = 4
 CHIPS = 4
@@ -505,11 +524,8 @@
     normal2,
     spread2,
     branch,
-    middle_grad,
     mcol,
     nl,
-    kvo,
-    qo,
     qi,
     whm,
     cosb,
@@ -537,7 +553,6 @@
     pn_yi,
     bgg,
     mig,
-    dob,
     doi,
     dos,
     sbo,
@@ -723,14 +738,20 @@
         for h in range(per):
             n = g * per + h
             tile = jnp.concatenate([of_head(1, n), of_head(2, n)], axis=1)
-            kvo[g, h] = jnp.where(low_half, turn(tile, cosine, sine), tile).astype(bf16)
+            rsx_out[h, g * rows : (g + 1) * rows, :] = jnp.where(
+                low_half, turn(tile, cosine, sine), tile
+            ).astype(bf16)
     here = pl.ds(z * rows, rows)
+
+    def out_of(ref, g):
+        return ref.at[:, pl.ds(g * rows, rows), :]
+
     zi = ids("kvz", 3)
     got_kv = []
     for k in (1, 2, 3):
         there = kvall.at[:, p, here, :]
-        got_kv.append(send(kvo.at[(z + k) % 4], there, zi + k - 1, zdev(k)))
-    kvall[:, p, here, :] = kvo[z]
+        got_kv.append(send(out_of(rsx_out, (z + k) % 4), there, zi + k - 1, zdev(k)))
+    kvall[:, p, here, :] = rsx_out[:, here, :]
 
     def over_plane(k):
         src = kvall.at[:, p, pl.ds(zfrom(k) * rows, rows), :]
@@ -741,12 +762,10 @@
     for g in range(GROUPS):
         n = g * per
         tile = turn(thirds[0][:, n * head : (n + 2) * head], cosine, sine) * scale
-        qo[g, 0] = tile.astype(bf16)
+        rso[0, g * rows : (g + 1) * rows, :] = tile.astype(bf16)
         tile = jnp.concatenate([of_head(0, n + 2), jnp.zeros((rows, head), f32)], axis=1)
-        qo[g, 1] = (turn(tile, cosine, sine) * scale).astype(bf16)
-    i = ids("q", 3)
-    got_q = [send(qo.at[(z + k) % 4], qi.at[z], i + k - 1, zdev(k)) for k in (1, 2, 3)]
-    qi[z] = qo[z]
+        rso[1, g * rows : (g + 1) * rows, :] = (turn(tile, cosine, sine) * scale).astype(bf16)
+    qi[z] = rso[:, here, :]
     for g in range(GROUPS):
         for h in range(per):
             a = g * gw + h * head
@@ -765,8 +784,8 @@
     for k in (1, 2, 3):
         got_kv[k - 1].wait_recv()
         over_plane(k)
-    i = ids("nl", 3)
-    got_nl = [send(nl.at[z], nl.at[z], i + k - 1, zdev(k)) for k in (1, 2, 3)]
+    i = ids("q", 3)
+    got_q = [send(out_of(rso, (z + k) % 4), qi.at[z], i + k - 1, zdev(k)) for k in (1, 2, 3)]
     kdi = ids("kvd", 4)
     remote(kvall.at[:, p], kvall.at[:, p], kdi, sib).start()
     for copy in got_q:
@@ -783,36 +802,35 @@
     ot[...] = jnp.zeros_like(ot)
 
     def forward(i, carry):
-        k, r = i // (2 * per), i % (2 * per)
-        h, away = r % per, r // per
+        k, away = i // 2, i % 2
         chunk = chip_of(k) * 2 + (c + away) % 2
 
-        @pl.when((r == 0) & (k > 0))
+        @pl.when((away == 0) & (k > 0))
         def _():
             for q in range(GROUPS):
                 block = kvall.at[:, chunk, pl.ds(q * rows, rows), :]
                 remote(block, block, kvi + (k - 1) * 4 + q, sib).wait_recv()
             remote(kvall.at[:, chunk], kvall.at[:, chunk], kdi + k, sib).start()
 
-        @pl.when(r == per)
+        @pl.when(away == 1)
         def _():
             remote(kvall.at[:, chunk], kvall.at[:, chunk], kdi + k, sib).wait_recv()
 
-        keys = kvall[h, chunk]
-        scores = dot(keys, qd[h], 1, 1)
-        before = mrun[h]
-        top = jnp.maximum(before, jnp.max(scores, axis=0, keepdims=True))
-        weights = jnp.exp(scores - top)
-        factor = jnp.exp(before - top)
-        rounded = weights.astype(bf16)
-        expd[h, chunk] = rounded
-        lrun[h] = lrun[h] * factor + column_sum(weights)
-        mrun[h] = top
-        tops[h, chunk] = top
-        ot[h] = ot[h] * factor + dot(keys, rounded, 0, 0)
+        scores = [dot(kvall[h, chunk], qd[h], 1, 1) for h in range(per)]
+        for h in range(per):
+            before = mrun[h]
+            top = jnp.maximum(before, jnp.max(scores[h], axis=0, keepdims=True))
+            weights = jnp.exp(scores[h] - top)
+            factor = jnp.exp(before - top)
+            rounded = weights.astype(bf16)
+            expd[h, chunk] = rounded
+            lrun[h] = lrun[h] * factor + column_sum(weights)
+            mrun[h] = top
+            tops[h, chunk] = top
+            ot[h] = ot[h] * factor + dot(kvall[h, chunk], rounded, 0, 0)
         return carry
 
-    lax.fori_loop(0, 2 * CHIPS * per, forward, 0)
+    lax.fori_loop(0, 2 * CHIPS, forward, 0)
 
     for h in range(per):
         ot[h] = ot[h] / lrun[h]
@@ -829,86 +847,109 @@
     rg3.wait_recv()
     weights[0].wait()
     for tb in range(tp_size):
-        ag[tb] = dot(rg[tb], down_w[...], 1, 1)
+        ag[tb] = dot(rg[tb], down_w[...], 1, 1).astype(bf16)
     for copy in got_mix:
         copy.wait_recv()
+    i = ids("nl", 3)
+    got_nl = [send(nl.at[z], nl.at[z], i + k - 1, zdev(k)) for k in (1, 2, 3)]
     weights[1].wait()
     weights[2].wait()
     total = dot(mi[0], out_w[0:gw, :], 0, 0)
     for g in range(1, GROUPS):
         total = total + dot(mi[g], out_w[g * gw : (g + 1) * gw, :], 0, 0)
-    i = ids("mig", 3)
-    to = ((t_sib, sib), (t_y, dev(1)), (t_ysib, ysib))
-    got_mig = [send(mi.at[at], mig.at[t], i + n, where) for n, (at, where) in enumerate(to)]
-    mig[t] = mi[t]
     branch[...] = total
     start[...] = start[...] + gate1 * total
     normal, spread = normalise(start[...])
     normal2[...] = normal
     spread2[...] = spread
     ng[t] = (normal * (gain2 * (1.0 + scale2)) + shift2).astype(bf16)
-    ng1, ng2, ngi = group_start(ng, "ng")
-
+    piece = rows // 2
+    halves = [pl.ds(n * piece, piece) for n in range(2)]
+
+    def to_group(buffer, name):
+        i = ids(name, 6)
+        got = []
+        for n, at in enumerate(halves):
+            src = buffer.at[t, at]
+            got.append((send(src, src, i + 3 * n, sib), send(src, src, i + 3 * n + 1, dev(1))))
+        return got, i
+
+    def pass_group(buffer, got, i, n):
+        got[n][1].wait_recv()
+        src = buffer.at[t_y, halves[n]]
+        return send(src, src, i + 3 * n + 2, sib)
+
+    got_ng, ngi = to_group(ng, "ng")
     inner, cubic = 0.7978845608028654, 0.044715
 
-    def feed(tb):
-        hidden = dot(ng[tb], up_w[...], 1, 0) + up_b
+    def feed(tb, n):
+        at = halves[n]
+        hidden = dot(ng[tb, at], up_w[...], 1, 0) + up_b
         square = hidden * hidden
         bent = jnp.tanh(inner * hidden * (1.0 + cubic * square))
         share = 0.5 * (1.0 + bent)
-        acts[tb] = (hidden * share).astype(bf16)
+        acts[tb, at] = (hidden * share).astype(bf16)
         slope = share + 0.5 * hidden * (1.0 - bent * bent) * (
             inner * (1.0 + 3.0 * cubic * square)
         )
-        hgs[tb] = (ag[tb] * slope).astype(bf16)
-        return dot(hgs[tb], up_w[...], 1, 1)
-
-    def group_sum(n, term, name, own_first, sib_first, y_first, ysib_first):
-        i = ids(name, 3)
-        if own_first is not None:
-            own_first()
-        pn_own[n] = term(t)
-        if sib_first is not None:
-            sib_first()
-        pn_so[n, 0] = term(t_sib).astype(bf16)
-        one = send(pn_so.at[n, 0], pn_si.at[n, 0], i, sib)
-        if ysib_first is not None:
-            y_first()
-            ysib_first()
-        pn_so[n, 1] = term(t_ysib).astype(bf16)
-        two = send(pn_so.at[n, 1], pn_si.at[n, 1], i + 1, sib)
-        mine = term(t_y)
+        back = (ag[tb, at].astype(f32) * slope).astype(bf16)
+        hgs[tb, at] = back
+        return dot(back, up_w[...], 1, 1)
+
+    def group_sum(m, term, name, n, one_ready, two_ready):
+        i, at = ids(name, 3), halves[n]
+        pn_own[m, at] = term(t, n)
+        one_ready()
+        pn_so[m, 0, at] = term(t_sib, n).astype(bf16)
+        one = send(pn_so.at[m, 0, at], pn_si.at[m, 0, at], i, sib)
+        two_ready()
+        pn_so[m, 1, at] = term(t_ysib, n).astype(bf16)
+        two = send(pn_so.at[m, 1, at], pn_si.at[m, 1, at], i + 1, sib)
+        mine = term(t_y, n)
         two.wait_recv()
-        pn_yo[n] = (mine + pn_si[n, 1].astype(f32)).astype(bf16)
-        three = send(pn_yo.at[n], pn_yi.at[n], i + 2, dev(1))
-
-        def finish():
+        pn_yo[m, at] = (mine + pn_si[m, 1, at].astype(f32)).astype(bf16)
+        three = send(pn_yo.at[m, at], pn_yi.at[m, at], i + 2, dev(1))
+        return one, three
+
+    def group_total(m, parts):
+        for one, three in parts:
             one.wait_recv()
             three.wait_recv()
-            return pn_own[n] + pn_si[n, 0].astype(f32) + pn_yi[n].astype(f32)
-
-        return finish
-
-    ng3 = []
-    finish_grad = group_sum(
-        0,
-        feed,
-        "pn",
-        None,
-        ng1.wait_recv,
-        lambda: ng3.append(group_pass(ng, ng2, ngi)),
-        lambda: ng3[0].wait_recv(),
-    )
+        return pn_own[m] + pn_si[m, 0].astype(f32) + pn_yi[m].astype(f32)
+
+    def nothing():
+        pass
+
+    back_parts = []
+    for n in range(2):
+        passed = []
+        back_parts.append(
+            group_sum(
+                0,
+                feed,
+                f"pn{n}",
+                n,
+                got_ng[n][0].wait_recv,
+                lambda: (
+                    passed.append(pass_group(ng, got_ng, ngi, n)),
+                    passed[0].wait_recv(),
+                ),
+            )
+        )
+    i = ids("mig", 3)
+    to = ((t_sib, sib), (t_y, dev(1)), (t_ysib, ysib))
+    got_mig = [send(mi.at[at], mig.at[t], i + n, where) for n, (at, where) in enumerate(to)]
+    mig[t] = mi[t]
     half_rows = width // 2
 
-    def exchange(buffer, incoming, parts, gathered, base, count, name):
+    def exchange(buffer, incoming, parts, gathered, base, count, cols, name):
         near, own = count // 2, count // 2 // GROUPS
         i = ids(name, 8)
-        src = buffer.at[pl.ds(base + (1 - x) * near, near)]
+        src = buffer.at[pl.ds(base + (1 - x) * near, near), cols]
         got = send(src, incoming, i, dev(2))
         yield
         got.wait_recv()
-        mine = buffer[pl.ds(base + x * near, near), :].astype(f32) + incoming[...].astype(f32)
+        mine = buffer[pl.ds(base + x * near, near), cols].astype(f32) + incoming[...].astype(f32)
         incoming[...] = mine.astype(bf16)
         beside = ((z + 1 - 2 * (z % 2)) * 2 + x, t)
         got = []
@@ -927,7 +968,7 @@
         mine = incoming[pl.ds(z * own, own), :].astype(f32) + parts[2].astype(f32)
 
         def place(d):
-            return gathered.at[pl.ds(base + x * near + d * own, own)]
+            return gathered.at[pl.ds(base + x * near + d * own, own), cols]
 
         src = place(z)
         src[...] = mine.astype(bf16)
@@ -938,115 +979,84 @@
         yield
         for copy in got:
             copy.wait_recv()
-        src = gathered.at[pl.ds(base + x * near, near)]
+        src = gathered.at[pl.ds(base + x * near, near), cols]
         got = send(src, src, i + 7, dev(2))
         yield
         got.wait_recv()
         yield
 
-    def exchange_of(m):
-        side = pl.ds(m * half_rows, half_rows)
-        return exchange(mbuf, msi.at[side], mz.at[m], mgat, m * width, width, f"m{m}")
-
-    def matrix(left, right):
-        return dot(left[...].reshape(line, width), right[...].reshape(line, width), 0, 0)
-
-    mbuf[width : 2 * width, :] = matrix(acts, rg).astype(bf16)
-    down_path = exchange_of(1)
-    next(down_path)
-
-    upstream = cot_ref[...].astype(f32)
-    n2g = finish_grad()
-    normal = normal2[...]
-    middle = normalise_back(n2g * (gain2 * (1.0 + scale2)), normal, spread2[...]) + upstream
-    bgg[t] = (middle * gate1).astype(bf16)
-    for g in range(GROUPS):
-        dob[g] = dot(out_w[g * gw : (g + 1) * gw, :], bgg[t], 1, 1).astype(bf16)
-    i = ids("do", 3)
-    got_do = [send(dob.at[(z + k) % 4], doi.at[z], i + k - 1, zdev(k)) for k in (1, 2, 3)]
-    bg1, bg2, bgi = group_start(bgg, "bg")
-    doi[z] = dob[z]
-    middle_grad[...] = middle
-    vec[3:4, :] = column_sum(middle * branch[...])
-    vec[4:5, :] = column_sum(n2g)
-    vec[5:6, :] = column_sum(n2g * normal)
-    mbuf[0:width, :] = matrix(ng, hgs).astype(bf16)
-    up_path = exchange_of(0)
-    next(up_path)
-    finish_result = group_sum(
-        1, lambda tb: dot(acts[tb], down_w[...], 1, 0), "res", None, None, None, None
-    )
-    bg3 = group_pass(bgg, bg2, bgi)
-    vec[8:9, :] = column_sum(hgs[...].reshape(line, width).astype(f32))
-    vec[9:16, :] = jnp.zeros((7, width), f32)
-    vec[7:8, :] = column_sum(rg[t].astype(f32))
-
-    for copy in got_do:
-        copy.wait_recv()
-    for h in range(per):
-        dos[h, 0:head, :] = jnp.zeros((head, line), bf16)
-        for zb in range(GROUPS):
-            dos[h, head : 2 * head, zb * rows : (zb + 1) * rows] = doi[
-                zb, h * head : (h + 1) * head, :
-            ]
-        delta[h] = column_sum(dos[h, head : 2 * head, :].astype(f32) * ot[h, head : 2 * head, :])
-    dq = ot
-    dq[...] = jnp.zeros_like(dq)
+    wide = width // 2
+    paths = {}
+
+    def weight_piece(name, m, n, left, right):
+        cols = pl.ds(n * wide, wide)
+        upper = right[:, :, n * wide : (n + 1) * wide].reshape(line, wide)
+        grad = dot(left[...].reshape(line, width), upper, 0, 0)
+        mbuf[m * width : (m + 1) * width, n * wide : (n + 1) * wide] = grad.astype(bf16)
+        incoming = msi.at[pl.ds(m * half_rows, half_rows), cols]
+        parts = mz.at[m, :, :, cols]
+        paths[name] = exchange(mbuf, incoming, parts, mgat, m * width, width, cols, name)
+        next(paths[name])
+
     sbx = ids("sb", 12)
     rsi_at = ids("rs", 9)
+    dq = ot
+    kept = {}
 
     def backward(i, carry):
-        h, r = i // (2 * CHIPS), i % (2 * CHIPS)
-        away, k = 1 - r // CHIPS, CHIPS - 1 - r % CHIPS
-        chunk = chip_of(k) * 2 + (c + away) % 2
-        keys = kvall[h, chunk]
-        factor = jnp.exp(tops[h, chunk] - lse[h])
-        scaled = (dos[h].astype(f32) * factor).astype(bf16)
-        prob_grad = dot(keys, scaled, 1, 0)
-        rounded = expd[h, chunk]
-        score_grad = (rounded.astype(f32) * (prob_grad - delta[h] * factor)).astype(bf16)
-        dq[h] = dq[h] + dot(keys, score_grad, 0, 0)
-        part = dot(score_grad, qd[h], 1, 0) + dot(rounded, scaled, 1, 1)
-        over = remote(sbo.at[k], sbi.at[h, k], sbx + h * CHIPS + k, sib)
+        h, r = i // CHIPS, i % CHIPS
+        away, upper = 1 - r // 2, 1 - r % 2
+        last = h // (per - 1)
+        ks = (2 * upper + 1, 2 * upper)
+        chunks = [chip_of(k) * 2 + (c + away) % 2 for k in ks]
+        factors = [jnp.exp(tops[h, chunk] - lse[h]) for chunk in chunks]
+        scaled = [(dos[h].astype(f32) * factor).astype(bf16) for factor in factors]
+        prob_grads = [dot(kvall[h, chunk], d, 1, 0) for chunk, d in zip(chunks, scaled)]
+        value_parts = [dot(expd[h, chunk], d, 1, 1) for chunk, d in zip(chunks, scaled)]
+        parts = []
+        for n, chunk in enumerate(chunks):
+            weight = expd[h, chunk].astype(f32)
+            score_grad = (weight * (prob_grads[n] - delta[h] * factors[n])).astype(bf16)
+            dq[h] = dq[h] + dot(kvall[h, chunk], score_grad, 0, 0)
+            parts.append(dot(score_grad, qd[h], 1, 0) + value_parts[n])
+        overs = [remote(sbo.at[k], sbi.at[h, k], sbx + h * CHIPS + k, sib) for k in ks]
 
         @pl.when((away == 1) & (h > 0))
         def _():
-            remote(sbo.at[k], sbi.at[h, k], sbx + (h - 1) * CHIPS + k, sib).wait_send()
+            for k in ks:
+                remote(sbo.at[k], sbi.at[h, k], sbx + (h - 1) * CHIPS + k, sib).wait_send()
 
         @pl.when(away == 1)
         def _():
-            sbo[k] = part.astype(bf16)
-            over.start()
+            for n, k in enumerate(ks):
+                sbo[k] = parts[n].astype(bf16)
+                overs[n].start()
+
+        @pl.when((away == 0) & (h > 0))
+        def _():
+            i = rsi_at + (h - 1) * 3 + upper
+            remote(rso.at[upper], rsi.at[h, upper], i, sib).wait_send()
 
         @pl.when(away == 0)
         def _():
-            over.wait_recv()
-            both = part + sbi[h, k].astype(f32)
-
-            @pl.when(k == 0)
+            overs[0].wait_recv()
+            rso[upper] = (parts[0] + sbi[h, ks[0]].astype(f32)).astype(bf16)
+            i = rsi_at + h * 3 + upper
+            remote(rso.at[upper], rsi.at[h, upper], i, dev(1 + 2 * upper * last)).start()
+            overs[1].wait_recv()
+            both = parts[1] + sbi[h, ks[1]].astype(f32)
+
+            @pl.when(upper == 0)
             def _():
                 dkv[h] = both
 
-            final = h // (per - 1)
-
-            @pl.when(k == 2)
+            @pl.when(upper == 1)
             def _():
                 rsx_out[h] = both.astype(bf16)
 
-            @pl.when((k == 2) & (final == 1))
+            @pl.when((upper == 1) & (last == 1))
             def _():
                 remote(rsx_out.at[h], rsx_in.at[h], rsi_at + h * 3 + 2, dev(2)).start()
-
-            odd = k // 2
-
-            @pl.when((k % 2 == 1) & (h > 0))
-            def _():
-                remote(rso.at[odd], rsi.at[h, odd], rsi_at + (h - 1) * 3 + odd, sib).wait_send()
-
-            @pl.when(k % 2 == 1)
-            def _():
-                rso[odd] = both.astype(bf16)
-                remote(rso.at[odd], rsi.at[h, odd], rsi_at + h * 3 + odd, dev(1 + 2 * odd * final)).start()
 
         return carry
 
@@ -1126,131 +1136,229 @@
         yield
 
     across = {}
-    backward_from(0, 8)
-    next(down_path)
-    bg1.wait_recv()
-    bg3.wait_recv()
-    for copy in got_mig:
-        copy.wait_recv()
-    grad = dot(mig[0], bgg[0], 1, 0)
-    for n in range(1, tp_size):
-        grad = grad + dot(mig[n], bgg[n], 1, 0)
-    wide = width // 2
-    wbuf[0:gw, :] = grad[:, 0:wide].astype(bf16)
-    wbuf[gw : 2 * gw, :] = grad[:, wide:width].astype(bf16)
-    out_path = exchange(wbuf, wsi, wz, wgt, 0, 2 * gw, "wo")
-    next(out_path)
-    result = finish_result() + down_b
-    o_out[...] = (start[...] + gate2 * result).astype(bf16)
-    vec[6:7, :] = column_sum(cot_ref[...].astype(f32) * result)
-    backward_from(8, 16)
-    across[0] = relay(0)
-    next(down_path)
-    next(up_path)
-    backward_from(16, 20)
-    across[1] = relay(1)
-    backward_from(20, 24)
-    across[2] = remote(rsx_out.at[per - 1], rsx_in.at[per - 1], rsi_at + per * 3 - 1, dev(2))
-    pending.append(across[2])
-    next(out_path)
-    next(down_path)
-    for copy in got_nl:
-        copy.wait_recv()
-    keys_back(0, pg1, kv_at[0])
-    keys_back(1, pg1, kv_at[1])
-    queries_back(dq[0, 0:head, :], dq[1, 0:head, :], pg1, q_at[0])
-    got_pg1 = scatter_rows(pg1, pgi1, "pg1")
-    first_path = projection(pg1, dwb1, dws1, dwc1, dwr1, wg1, "w1")
-    next(first_path)
-    keys_back(2, pg2, kv_at[2] - split)
-    queries_back(dq[2, 0:head, :], jnp.zeros((head, line), f32), pg2, q_at[1] - split)
-    got_pg2 = scatter_rows(pg2, pgi2, "pg2")
-    second_path = projection(pg2, dwb2, dws2, dwc2, dwr2, wg2, "w2")
-    next(second_path)
-    next(first_path)
-    next(up_path)
-    next(out_path)
-    next(second_path)
-    next(first_path)
-    next(down_path)
-    next(second_path)
-    next(up_path)
-    next(out_path)
-    for copy in got_pg1:
-        copy.wait_recv()
-    n1g = dot(pgi1[0], whm[0, :, 0:split], 1, 1)
-    for g in range(1, GROUPS):
-        n1g = n1g + dot(pgi1[g], whm[g, :, 0:split], 1, 1)
-    for copy in got_pg2:
-        copy.wait_recv()
-    for g in range(GROUPS):
-        n1g = n1g + dot(pgi2[g], whm[g, :, split : split + 4 * head], 1, 1)
-    normal = normal1[...]
-    vec[1:2, :] = column_sum(n1g)
-    vec[2:3, :] = column_sum(n1g * normal)
-    grad = normalise_back(n1g * (gain1 * (1.0 + scale1)), normal, spread1[...]) + middle_grad[...]
-    o_in[...] = grad
-    vec[0:1, :] = column_sum(grad * mcol[...])
-    vpl[chip] = vec[...]
-    i = ids("vp", 3)
-    got_vp = [send(vec, vpl.at[chip], i + k - 1, dev(k)) for k in (1, 2, 3)]
-    next(first_path)
-    next(down_path)
-    next(out_path)
-    next(second_path)
-    for copy in got_vp:
-        copy.wait_recv()
-    vzs[z, 0:8] = (vpl[0, 0:8] + vpl[1, 0:8]) + (vpl[2, 0:8] + vpl[3, 0:8])
-    vzs[z, 8:16] = vpl[y, 8:16] + vpl[2 + y, 8:16]
-    iv = ids("vz", 3)
-    got_vz = [send(vzs.at[z], vzs.at[z], iv + k - 1, zdev(k)) for k in (1, 2, 3)]
-    next(up_path)
-    next(out_path)
-    next(first_path)
-    next(second_path)
-    for copy in got_vz:
-        copy.wait_recv()
-    vco[c] = (vzs[0] + vzs[1]) + (vzs[2] + vzs[3])
-    got_vc = send(vco.at[c], vco.at[c], ids("vc", 1), sib)
-    next(out_path)
-    og[t] = wgt[...]
-    og1, og2, ogi = group_start(og, "og")
-    next(up_path)
-    next(first_path)
-    next(second_path)
-    got_vc.wait_recv()
-    sums = vco[0] + vco[1]
-    o_vec[0:1, :] = sums[0:1, :]
-    o_vec[1:2, :] = sums[2:3, :] * (1.0 + scale1)
-    o_vec[2:3, :] = sums[5:6, :] * (1.0 + scale2)
-    o_vec[3:4, :] = sums[7:8, :]
-    o_vec[4:5, :] = vco[c, 8:9, :]
-    o_vec[5:8, :] = jnp.zeros((3, width), f32)
-    o_vec[8:9, :] = sums[1:2, :]
-    o_vec[9:10, :] = sums[2:3, :] * gain1
-    o_vec[10:11, :] = sums[3:4, :]
-    o_vec[11:12, :] = sums[4:5, :]
-    o_vec[12:13, :] = sums[5:6, :] * gain2
-    o_vec[13:14, :] = sums[6:7, :]
-    o_vec[14:16, :] = jnp.zeros((2, width), f32)
-    og3 = group_pass(og, og2, ogi)
     copies = []
 
     def write(src, dst):
         copies.append(pltpu.make_async_copy(src, dst, ls.at[len(copies)]))
         copies[-1].start()
 
-    next(down_path)
-    write(mgat.at[width : 2 * width], o_mlp.at[width : 2 * width])
-    next(first_path)
-    write(wg1, o_qkv1)
-    next(second_path)
-    write(wg2, o_qkv2)
-    og1.wait_recv()
-    og3.wait_recv()
-    write(og, o_ow)
-    next(up_path)
-    write(mgat.at[0:width], o_mlp.at[0:width])
+    def second_norm_back():
+        n2g = group_total(0, back_parts)
+        sent = got_kv + got_q + got_mix
+        for copy in sent:
+            copy.wait_send()
+        pending[:] = [copy for copy in pending if not any(copy is other for other in sent)]
+        normal = normal2[...]
+        middle = normalise_back(n2g * (gain2 * (1.0 + scale2)), normal, spread2[...])
+        middle = middle + cot_ref[...].astype(f32)
+        bgg[t] = (middle * gate1).astype(bf16)
+        for g in range(GROUPS):
+            mtb[g] = dot(out_w[g * gw : (g + 1) * gw, :], bgg[t], 1, 1).astype(bf16)
+        i = ids("do", 3)
+        kept["do"] = [send(mtb.at[(z + k) % 4], doi.at[z], i + k - 1, zdev(k)) for k in (1, 2, 3)]
+        kept["bg"] = group_start(bgg, "bg")
+        doi[z] = mtb[z]
+        normal2[...] = middle
+        vec[3:4, :] = column_sum(middle * branch[...])
+        vec[4:5, :] = column_sum(n2g)
+        vec[5:6, :] = column_sum(n2g * normal)
+
+    def result_term(tb, n):
+        return dot(acts[tb, halves[n]], down_w[...], 1, 0)
+
+    def result_start():
+        kept["res"] = [
+            group_sum(1, result_term, f"res{n}", n, nothing, nothing) for n in range(2)
+        ]
+        vec[8:9, :] = column_sum(hgs[...].reshape(line, width).astype(f32))
+        vec[9:16, :] = jnp.zeros((7, width), f32)
+        vec[7:8, :] = column_sum(rg[t].astype(f32))
+
+    def result_end():
+        result = group_total(1, kept["res"]) + down_b
+        o_out[...] = (start[...] + gate2 * result).astype(bf16)
+        vec[6:7, :] = column_sum(cot_ref[...].astype(f32) * result)
+
+    def branch_pass():
+        one, two, i = kept["bg"]
+        kept["bg3"] = group_pass(bgg, two, i)
+
+    def out_weight_grad():
+        kept["bg"][0].wait_recv()
+        kept["bg3"].wait_recv()
+        for copy in got_mig:
+            copy.wait_recv()
+        grad = dot(mig[0], bgg[0], 1, 0)
+        for n in range(1, tp_size):
+            grad = grad + dot(mig[n], bgg[n], 1, 0)
+        wbuf[0:gw, :] = grad[:, 0:wide].astype(bf16)
+        wbuf[gw : 2 * gw, :] = grad[:, wide:width].astype(bf16)
+        paths["o"] = exchange(wbuf, wsi, wz, wgt, 0, 2 * gw, pl.ds(0, wide), "wo")
+        next(paths["o"])
+
+    def backward_first():
+        for copy in kept["do"]:
+            copy.wait_recv()
+        for h in range(per):
+            dos[h, 0:head, :] = jnp.zeros((head, line), bf16)
+            for zb in range(GROUPS):
+                dos[h, head : 2 * head, zb * rows : (zb + 1) * rows] = doi[
+                    zb, h * head : (h + 1) * head, :
+                ]
+            delta[h] = column_sum(
+                dos[h, head : 2 * head, :].astype(f32) * ot[h, head : 2 * head, :]
+            )
+        dq[...] = jnp.zeros_like(dq)
+        backward_from(0, 4)
+
+    def backward_last():
+        backward_from(10, 12)
+        across[2] = remote(rsx_out.at[per - 1], rsx_in.at[per - 1], rsi_at + per * 3 - 1, dev(2))
+        pending.append(across[2])
+
+    def relay_of(h):
+        across[h] = relay(h)
+
+    kept["nl"] = got_nl
+
+    def portion_one():
+        for copy in kept.pop("nl", []):
+            copy.wait_recv()
+        keys_back(0, pg1, kv_at[0])
+        keys_back(1, pg1, kv_at[1])
+        queries_back(dq[0, 0:head, :], dq[1, 0:head, :], pg1, q_at[0])
+        kept["pg1"] = scatter_rows(pg1, pgi1, "pg1")
+        paths["w1"] = projection(pg1, dwb1, dws1, dwc1, dwr1, wg1, "w1")
+        next(paths["w1"])
+
+    def portion_two():
+        for copy in kept.pop("nl", []):
+            copy.wait_recv()
+        keys_back(2, pg2, kv_at[2] - split)
+        queries_back(dq[2, 0:head, :], jnp.zeros((head, line), f32), pg2, q_at[1] - split)
+        kept["pg2"] = scatter_rows(pg2, pgi2, "pg2")
+        paths["w2"] = projection(pg2, dwb2, dws2, dwc2, dwr2, wg2, "w2")
+        next(paths["w2"])
+
+    def first_norm_back():
+        for copy in kept["pg1"]:
+            copy.wait_recv()
+        n1g = dot(pgi1[0], whm[0, :, 0:split], 1, 1)
+        for g in range(1, GROUPS):
+            n1g = n1g + dot(pgi1[g], whm[g, :, 0:split], 1, 1)
+        for copy in kept["pg2"]:
+            copy.wait_recv()
+        for g in range(GROUPS):
+            n1g = n1g + dot(pgi2[g], whm[g, :, split : split + 4 * head], 1, 1)
+        normal = normal1[...]
+        vec[1:2, :] = column_sum(n1g)
+        vec[2:3, :] = column_sum(n1g * normal)
+        grad = normalise_back(n1g * (gain1 * (1.0 + scale1)), normal, spread1[...])
+        grad = grad + normal2[...]
+        o_in[...] = grad
+        vec[0:1, :] = column_sum(grad * mcol[...])
+        vpl[chip] = vec[...]
+        i = ids("vp", 3)
+        kept["vp"] = [send(vec, vpl.at[chip], i + k - 1, dev(k)) for k in (1, 2, 3)]
+
+    def vectors_plane():
+        for copy in kept["vp"]:
+            copy.wait_recv()
+        vzs[z, 0:8] = (vpl[0, 0:8] + vpl[1, 0:8]) + (vpl[2, 0:8] + vpl[3, 0:8])
+        vzs[z, 8:16] = vpl[y, 8:16] + vpl[2 + y, 8:16]
+        i = ids("vz", 3)
+        kept["vz"] = [send(vzs.at[z], vzs.at[z], i + k - 1, zdev(k)) for k in (1, 2, 3)]
+
+    def vectors_line():
+        for copy in kept["vz"]:
+            copy.wait_recv()
+        vco[c] = (vzs[0] + vzs[1]) + (vzs[2] + vzs[3])
+        kept["vc"] = send(vco.at[c], vco.at[c], ids("vc", 1), sib)
+
+    def vectors_end():
+        kept["vc"].wait_recv()
+        sums = vco[0] + vco[1]
+        o_vec[0:1, :] = sums[0:1, :]
+        o_vec[1:2, :] = sums[2:3, :] * (1.0 + scale1)
+        o_vec[2:3, :] = sums[5:6, :] * (1.0 + scale2)
+        o_vec[3:4, :] = sums[7:8, :]
+        o_vec[4:5, :] = vco[c, 8:9, :]
+        o_vec[5:8, :] = jnp.zeros((3, width), f32)
+        o_vec[8:9, :] = sums[1:2, :]
+        o_vec[9:10, :] = sums[2:3, :] * gain1
+        o_vec[10:11, :] = sums[3:4, :]
+        o_vec[11:12, :] = sums[4:5, :]
+        o_vec[12:13, :] = sums[5:6, :] * gain2
+        o_vec[13:14, :] = sums[6:7, :]
+        o_vec[14:16, :] = jnp.zeros((2, width), f32)
+
+    def out_start():
+        og[t] = wgt[...]
+        kept["og"] = group_start(og, "og")
+
+    def out_pass():
+        one, two, i = kept["og"]
+        kept["og3"] = group_pass(og, two, i)
+
+    def out_end():
+        kept["og"][0].wait_recv()
+        kept["og3"].wait_recv()
+        write(og, o_ow)
+
+    finished = []
+
+    def step_of(path, last):
+        def run():
+            next(paths[path])
+            if not last:
+                return
+            if path == "w1":
+                write(wg1, o_qkv1)
+            elif path == "w2":
+                write(wg2, o_qkv2)
+            elif path != "o":
+                finished.append(path[0])
+                if finished.count(path[0]) == 2:
+                    at = pl.ds(0 if path[0] == "u" else width, width)
+                    write(mgat.at[at], o_mlp.at[at])
+
+        return run
+
+    steps = {
+        "d1_dw": lambda: weight_piece("d1", 1, 0, acts, rg),
+        "d2_dw": lambda: weight_piece("d2", 1, 1, acts, rg),
+        "u1_dw": lambda: weight_piece("u1", 0, 0, ng, hgs),
+        "u2_dw": lambda: weight_piece("u2", 0, 1, ng, hgs),
+        "ln2b": second_norm_back,
+        "res": result_start,
+        "resfin": result_end,
+        "bgp": branch_pass,
+        "wo": out_weight_grad,
+        "L1": backward_first,
+        "L2": lambda: backward_from(4, 8),
+        "L3a": lambda: backward_from(8, 10),
+        "L3b": backward_last,
+        "rel0": lambda: relay_of(0),
+        "rel1": lambda: relay_of(1),
+        "por1": portion_one,
+        "por2": portion_two,
+        "n1g": first_norm_back,
+        "v1": vectors_plane,
+        "v2": vectors_line,
+        "v3": vectors_end,
+        "og": out_start,
+        "og2": out_pass,
+        "og3": out_end,
+    }
+    for path in ("d1", "d2", "u1", "u2", "o"):
+        for part in ("1", "2", "3", "4", "5", "end"):
+            steps[path + "_" + part] = step_of(path, part == "end")
+    for path in ("w1", "w2"):
+        for part in ("a", "b", "c", "d", "e", "end"):
+            steps[path + "_" + part] = step_of(path, part == "end")
+    for batch in ORDER:
+        for name in batch.split():
+            steps[name]()
     for copy in pending:
         copy.wait_send()
     for k in range(CHIPS):
@@ -1342,11 +1450,8 @@
             V((rows, width), f32),
             V((rows, 1), f32),
             V((rows, width), f32),
-            V((rows, width), f32),
             V((rows, 1), f32),
             V((GROUPS, rows, width), bf16),
-            V((GROUPS, per, rows, 2 * head), bf16),
-            V((GROUPS, 2, rows, 2 * head), bf16),
             V((GROUPS, 2, rows, 2 * head), bf16),
             V((GROUPS, width, packed), bf16),
             V((GROUPS, rows, 2 * head), f32),
@@ -1366,7 +1471,7 @@
             V((tp_size, rows, width), bf16),
             V((tp_size, rows, width), bf16),
             V((tp_size, rows, width), bf16),
-            V((tp_size, rows, width), f32),
+            V((tp_size, rows, width), bf16),
             V((2, rows, width), f32),
             V((2, 2, rows, width), bf16),
             V((2, 2, rows, width), bf16),
@@ -1374,7 +1479,6 @@
             V((2, rows, width), bf16),
             V((tp_size, rows, width), bf16),
             V((tp_size, gw, rows), bf16),
-            V((GROUPS, gw, rows), bf16),
             V((GROUPS, gw, rows), bf16),
             V((per, 2 * head, line), bf16),
             V((CHIPS, line, 2 * head), bf16),
@@ -1411,8 +1515,8 @@
             V((CHIPS, 16, width), f32),
             V((GROUPS, 16, width), f32),
             V((2, 16, width), f32),
-            pltpu.SemaphoreType.DMA((160,)),
-            pltpu.SemaphoreType.DMA((160,)),
+            pltpu.SemaphoreType.DMA((192,)),
+            pltpu.SemaphoreType.DMA((192,)),
             pltpu.SemaphoreType.DMA((20,)),
         ],
         compiler_params=pltpu.CompilerParams(

time: 200 us -> 173 us (0.86)
  Pallas kernels: 197 us -> 171 us
    pallas_call x1, Pallas kernels: 186 us -> 160 us  [fused_device(): pl.pallas_call(functools.partial(fused_kernel, tp_size), out_shape=[jax.S...]
where the time goes in v4:
time: 173 us
  Pallas kernels  171 us (99%)
  between operations  2.13 us (1%)
    pallas_call x1, Pallas kernels, fused_device(): pl.pallas_call(functools.partial(fused_kernel, tp_size), out_shape=[jax.S...  160 us
    pallas_call x1, Pallas kernels, fused_device(): pl.pallas_call(functools.partial(finish_kernel, per, head), grid=(steps,)...  11.1 us

profile of v4, /device:TPU:0, one launch (start us, length us, event | category | flops | bytes accessed | tf_op | source)
XLA Modules:
  0.0 172.9 jit_solution(15864113081402918884)
XLA Ops:
  1.9 159.7 %shard_map.273 = (bf16[128,768]{1,0:T(8,128)(2,1)}, f32[128,768]{1,0:T(8,128)}, f32[16,768]{1,0:T(8,128)}, bf16[4,4,2,96,384]{4,3,2,1,0:T(8,128)(2,1)}, bf16[4,4...) custom-call(s32[1]{0:T(128)S(6)} %copy.31.prefix_ref, ...), custom_call_target="tpu_custom_call" | custom-call | tf_op jit(solution)/shard_map/pallas_call | solution.py:1427
  161.6 11.1 %shard_map.274 = (bf16[128,768]{1,0:T(8,128)(2,1)}, f32[128,768]{1,0:T(8,128)}, f32[768]{0:T(1024)}, f32[768]{0:T(1024)}, f32[768]{0:T(1024)}, /*index=5*/f32[12...) custom-call(s32[1]{0:T(128)S(6)} %copy.32.timestep_ref, ...), custom_call_target="tpu_custom_call" | custom-call | tf_op jit(solution)/shard_map/pallas_call | solution.py:1556
